TPU v7x, 128 devices: a whole 4x4x4 slice. The times are simulated.
128 devices in a mesh: seq: 16 (over z, x), exp: 8 (over y, core).
Axes of the slice: x: 4, y: 4, z: 4, core: 2. Of those that a mesh axis runs over, the one named last changes fastest.
Arguments:
- query_states: bfloat16 [8, 2048, 4096], P('exp', 'seq'), may hold values from -8 to 8
- key_states: bfloat16 [8, 2048, 1024], P('exp', 'seq'), may hold values from -8 to 8
- value_states: bfloat16 [8, 2048, 1024], P('exp', 'seq'), may hold values from -6 to 6
- residual: bfloat16 [8, 2048, 3072], P('exp', 'seq'), may hold values from -6 to 6
- out_proj: bfloat16 [4096, 3072], P('seq'), may hold values from -0.09375 to 0.09375
- norm_gain: float32 [3072], replicated, may hold values from 0.25 to 1.75
- router: float32 [3072, 8], replicated, may hold values from -0.21875 to 0.21875
- w_gate: bfloat16 [8, 3072, 8192], P('exp', None, 'seq'), may hold values from -0.109375 to 0.109375
- w_up: bfloat16 [8, 3072, 8192], P('exp', None, 'seq'), may hold values from -0.109375 to 0.109375
- w_down: bfloat16 [8, 8192, 3072], P('exp', 'seq'), may hold values from -0.0625 to 0.0625
- reward_head: float32 [3072], replicated, may hold values from -5 to 5
- lengths: int32 [8, 2], P('exp'), may hold values from 512 to 1536, as said below
- routes: int32 [8, 2048, 2], P('exp', 'seq'), may hold values from 0 to 7, all different within a row; in each aligned block of 128 rows (0 to 127, 128 to 255, ..., all dimensions but the last counted through in order) at most 34 rows name the same one
- pair_list: int32 [8, 4, 2], replicated, may hold values from 0 to 1, as said below
Outputs:
- rewards: float32 [8, 2], replicated
- pair_loss: float32 [], replicated
- grad_head: float32 [3072], replicated
- grad_down: bfloat16 [8, 8192, 3072], P('exp', 'seq')
Inputs may be any that keep to these rules, and one draw needn't show every extreme that they name: Each group's lengths sum to 2048. `routes`: within the 128 tokens of one device (aligned blocks), each expert is named by at most 34 tokens, a bound that some block reaches; a token's two experts differ. `pair_list`: each judgment names two different responses of its group.
All inputs are finite; a program needn't handle non-finite values.
Results may differ from a plain program's by a relative error of at most 0.023.
Values may be sent and summed in bfloat16 or wider, within the bound.
A program may use at most 192 MiB of HBM per device.

v0:
```python
import jax
import jax.numpy as jnp
from jax import lax
from jax.sharding import PartitionSpec as P

D = 3072
Q_HEADS = 32
KV_HEADS = 8
HEAD_DIM = 128
SEQS = 2


def softmax_block(query_block, key_all, value_all, allowed):
    scores = jnp.einsum(
        "qhd,kd->hqk", query_block, key_all, preferred_element_type=jnp.float32
    ) * HEAD_DIM ** (-0.5)
    scores = jnp.where(allowed[None, :, :], scores, -1e30)
    largest = jnp.max(scores, axis=2, keepdims=True)
    exponent = jnp.exp(scores - largest)
    weights = (exponent / jnp.sum(exponent, axis=2, keepdims=True)).astype(jnp.bfloat16)
    return jnp.einsum("hqk,kd->qhd", weights, value_all, preferred_element_type=jnp.float32).astype(
        jnp.bfloat16
    )


def expert_terms(row_block, share_block, stream_ids, gate_cols, up_cols, streams):
    gate_vals = jnp.dot(row_block, gate_cols, preferred_element_type=jnp.float32)
    up_vals = jnp.dot(row_block, up_cols, preferred_element_type=jnp.float32)
    activity = jax.nn.silu(gate_vals) * up_vals
    stream_hot = (stream_ids[:, None] == jnp.arange(streams, dtype=jnp.int32)[None, :]).astype(
        jnp.float32
    )
    spread = (stream_hot[:, :, None] * share_block.astype(jnp.float32)[:, None, :]).reshape(
        row_block.shape[0], streams * SEQS
    )
    return jnp.einsum("rb,rf->bf", spread, activity, precision=lax.Precision.HIGHEST)


def per_device(
    query_states,
    key_states,
    value_states,
    residual,
    out_proj,
    norm_gain,
    router,
    w_gate,
    w_up,
    w_down,
    reward_head,
    lengths,
    routes,
    pair_list,
):
    highest = lax.Precision.HIGHEST
    seq_count = lax.axis_size("seq")
    exp_count = lax.axis_size("exp")
    tok_rows = residual.shape[1]
    seq_rows = tok_rows * seq_count
    heads_dev = Q_HEADS // seq_count
    repeat_kv = seq_count // KV_HEADS
    experts = router.shape[1]
    capacity = tok_rows * 34 // (16 * experts)
    query_local = query_states[0]
    key_local = jnp.repeat(key_states[0].reshape(tok_rows, KV_HEADS, HEAD_DIM), repeat_kv, axis=1)
    value_local = jnp.repeat(
        value_states[0].reshape(tok_rows, KV_HEADS, HEAD_DIM), repeat_kv, axis=1
    )
    paired = jnp.stack([key_local, value_local], axis=2).reshape(tok_rows, seq_count * 2 * HEAD_DIM)
    query_heads, paired_heads = (
        lax.all_to_all(query_local, "seq", split_axis=1, concat_axis=0, tiled=True),
        lax.all_to_all(paired, "seq", split_axis=1, concat_axis=0, tiled=True),
    )
    key_all = paired_heads[:, :HEAD_DIM]
    value_all = paired_heads[:, HEAD_DIM:]
    boundary = jnp.cumsum(lengths[0])
    position = jnp.arange(seq_rows, dtype=jnp.int32)
    segment = jnp.sum((position[:, None] >= boundary[None, :]).astype(jnp.int32), axis=1)
    block_rows = min(512, seq_rows)
    block_count = seq_rows // block_rows
    query_blocks = query_heads.reshape(block_count, block_rows, heads_dev, HEAD_DIM)

    def attend(operands):
        query_block, first_row = operands
        row_place = first_row + jnp.arange(block_rows, dtype=jnp.int32)
        row_segment = lax.dynamic_slice_in_dim(segment, first_row, block_rows)
        allowed = jnp.logical_and(
            row_place[:, None] >= position[None, :], row_segment[:, None] == segment[None, :]
        )
        return softmax_block(query_block, key_all, value_all, allowed)

    attended = lax.map(
        attend, (query_blocks, jnp.arange(block_count, dtype=jnp.int32) * block_rows)
    )
    attended = attended.reshape(seq_rows, heads_dev * HEAD_DIM)
    mixed = lax.psum_scatter(
        jnp.dot(attended, out_proj, preferred_element_type=jnp.float32).astype(jnp.bfloat16),
        "seq",
        scatter_dimension=0,
        tiled=True,
    ).astype(jnp.float32)
    hidden_in = residual[0].astype(jnp.float32) + mixed
    scale_row = lax.rsqrt(jnp.mean(hidden_in * hidden_in, axis=1, keepdims=True) + 1e-05)
    normed = (hidden_in * scale_row * norm_gain[None, :]).astype(jnp.bfloat16)
    logits = jnp.dot(normed.astype(jnp.float32), router, precision=highest)
    route_local = routes[0]
    expert_range = jnp.arange(experts, dtype=jnp.int32)
    first_hot = (route_local[:, 0:1] == expert_range[None, :]).astype(jnp.float32)
    second_hot = (route_local[:, 1:2] == expert_range[None, :]).astype(jnp.float32)
    first_logit = jnp.sum(first_hot * logits, axis=1)
    second_logit = jnp.sum(second_hot * logits, axis=1)
    gate_first = jax.nn.sigmoid(first_logit - second_logit)
    gate_second = jax.nn.sigmoid(second_logit - first_logit)
    my_seq = lax.axis_index("seq")
    my_stream = lax.axis_index("exp")
    own_segment = lax.dynamic_slice_in_dim(segment, my_seq * tok_rows, tok_rows)
    segment_hot = (own_segment[:, None] == jnp.arange(SEQS, dtype=jnp.int32)[None, :]).astype(
        jnp.float32
    )
    own_length = jnp.sum(segment_hot * lengths[0].astype(jnp.float32)[None, :], axis=1)
    slot_weight = (
        jnp.stack([gate_first / own_length, gate_second / own_length], axis=1)
        .astype(jnp.bfloat16)
        .reshape(-1)
    )
    expert_flat = route_local.reshape(-1)
    assign_hot = (expert_flat[:, None] == expert_range[None, :]).astype(jnp.int32)
    slot_rank = jnp.sum((jnp.cumsum(assign_hot, axis=0) - 1) * assign_hot, axis=1)
    slot_index = expert_flat * capacity + slot_rank
    slot_hot = slot_index[:, None] == jnp.arange(experts * capacity, dtype=jnp.int32)[None, :]
    token_slots = jnp.any(slot_hot.reshape(tok_rows, 2, experts * capacity), axis=1).astype(
        jnp.bfloat16
    )
    slot_rows = (
        jnp.einsum("ts,td->sd", token_slots, normed, preferred_element_type=jnp.float32)
        .astype(jnp.bfloat16)
        .reshape(experts, capacity, D)
    )
    pair_segment = jnp.repeat(segment_hot, 2, axis=0)
    weighted_slots = slot_hot.astype(jnp.float32) * slot_weight.astype(jnp.float32)[:, None]
    slot_share = (
        jnp.einsum("as,aq->sq", weighted_slots, pair_segment, precision=highest)
        .astype(jnp.bfloat16)
        .reshape(experts, capacity, SEQS)
    )
    received_rows, received_share = (
        lax.all_to_all(slot_rows, "exp", split_axis=0, concat_axis=0, tiled=True),
        lax.all_to_all(slot_share, "exp", split_axis=0, concat_axis=0, tiled=True),
    )
    flat_rows = received_rows.reshape(exp_count * capacity, D)
    flat_share = received_share.reshape(exp_count * capacity, SEQS)
    pieces = (
        lax.all_gather(flat_rows, "seq", axis=0, tiled=True),
        lax.all_gather(flat_share, "seq", axis=0, tiled=True),
    )
    row_total = pieces[0].shape[0]
    stream_ids = jnp.arange(row_total, dtype=jnp.int32) // capacity % exp_count
    hidden_sums = expert_terms(pieces[0], pieces[1], stream_ids, w_gate[0], w_up[0], exp_count)
    moved = jnp.dot(hidden_sums, w_down[0].astype(jnp.float32), precision=highest)
    pool_weight = segment_hot / own_length[:, None]
    pooled_own = jnp.einsum("tq,td->qd", pool_weight, hidden_in, precision=highest)
    stream_hot = (jnp.arange(exp_count, dtype=jnp.int32) == my_stream).astype(jnp.float32)
    pooled_part = (stream_hot[:, None, None] * pooled_own[None, :, :]).reshape(
        exp_count * SEQS, D
    ) + moved
    pooled = lax.psum(pooled_part, ("seq", "exp"))
    rewards = jnp.dot(pooled, reward_head, precision=highest).reshape(exp_count, SEQS)
    chosen_index = pair_list[:, :, 0]
    rejected_index = pair_list[:, :, 1]
    response_range = jnp.arange(SEQS, dtype=jnp.int32)
    chosen_hot = (chosen_index[:, :, None] == response_range).astype(jnp.float32)
    rejected_hot = (rejected_index[:, :, None] == response_range).astype(jnp.float32)
    margin = jnp.sum(chosen_hot * rewards[:, None, :], axis=2) - jnp.sum(
        rejected_hot * rewards[:, None, :], axis=2
    )
    pair_loss = jnp.mean(jnp.logaddexp(0.0, -margin))
    factor = -jax.nn.sigmoid(-margin) / (exp_count * pair_list.shape[1])
    reward_grad = jnp.sum(factor[:, :, None] * (chosen_hot - rejected_hot), axis=1).reshape(-1)
    rewards, pair_loss, reward_grad = (rewards, pair_loss, reward_grad)
    grad_head = jnp.dot(reward_grad, pooled, precision=highest)
    weighted = jnp.dot(reward_grad, hidden_sums, precision=highest)
    grad_down = (weighted[:, None] * reward_head[None, :]).astype(jnp.bfloat16)[None]
    return (rewards, pair_loss, grad_head, grad_down)


def solution(mesh):
    placed = (
        P("exp", "seq", None),
        P("exp", "seq", None),
        P("exp", "seq", None),
        P("exp", "seq", None),
        P("seq", None),
        P(),
        P(),
        P("exp", None, "seq"),
        P("exp", None, "seq"),
        P("exp", "seq", None),
        P(),
        P("exp", None),
        P("exp", "seq", None),
        P(),
    )
    return jax.shard_map(
        per_device,
        mesh=mesh,
        in_specs=placed,
        out_specs=(P(), P(), P(), P("exp", "seq", None)),
        check_vma=False,
    )
```

profile of v0, /device:TPU:0, one launch (start us, length us, event | category | flops | bytes accessed | tf_op | source)
XLA Modules:
  0.0 654.3 jit_solution(8937122575050651619)
XLA Ops:
  7.2 1.1 copy.124
  8.4 1.0 copy.125
  9.6 1.1 pad_maximum_fusion
  10.7 2.3 copy.104
  13.0 8.1 %all-to-all-start.1 = ((bf16[128,16,256]{0,2,1:T(8,128)(2,1)}), bf16[128,16,256]{0,2,1:T(8,128)(2,1)}, u32[]{:S(2)}, u32[]{:S(2)}) async-start(bf16[128,16,256]{0,2,1:T(8,128)(2,1)} %bitcast.140), calls=%async_computation.1 | async-start | bytes 2097152 | tf_op jit(solution)/shard_map/all_to_all | solution.py:72
  21.1 1.5 copy.123
  22.6 1.4 copy.101
  24.0 14.8 %all-to-all-done.1 = bf16[128,16,256]{0,2,1:T(8,128)(2,1)} async-done(((bf16[128,16,256]{0,2,1:T(8,128)(2,1)}), bf16[128,16,256]{0,2,1:T(8,128)(2,1)}, u32[]{:S(2)}, u32[]{:S(2)}) %all-to-all-start.1) | async-done | bytes 1048608 | tf_op jit(solution)/shard_map/all_to_all | solution.py:72
  38.8 4.3 all-to-all-start
  43.5 2.3 copy.105
  45.8 2.2 fusion.57
  48.0 11.0 %all-to-all-done = bf16[128,16,256]{2,0,1:T(8,128)(2,1)} async-done(((bf16[128,16,256]{2,0,1:T(8,128)(2,1)}), bf16[128,16,256]{2,0,1:T(8,128)(2,1)}, u32[]{:S(2)}, u32[]{:S(2)}) %all-to-all-start) | async-done | bytes 1048608 | tf_op jit(solution)/shard_map/all_to_all | solution.py:71
  59.1 2.2 reshape.381
  61.3 79.6 %while.11 = (s32[]{:T(128)}, bf16[4,512,2,128]{3,2,1,0:T(2,128)(2,1)}, s32[4]{0:T(128)S(1)}, s32[2048]{0:T(1024)S(1)}, bf16[4,512,2,128]{3,2,1,0:T(2,128)(2,1)},...) while((s32[]{:T(128)}, ...), condition=%wide.region_6.7_spmd.clone, body=%wide.region_3.6_spmd.clone.sunk | while | flops 1089604096 | bytes 21522604 | solution.py:92
  63.8 0.6 iota_add_fusion.2
  64.6 1.1 constant_dynamic-slice_fusion.2
  65.7 2.0 fusion.86
  67.7 7.8 %fusion.87 = (f32[2,512]{1,0:T(2,128)S(1)}, f32[2,512,2048]{2,1,0:T(8,128)}) fusion(pred[512,2048]{1,0:T(8,128)(4,1)} %fusion.86, bf16[2048,128]{1,0:T(8,128)(2,1)} %get-tuple-element.235, bf16[1,512,2,128]{3,2,1,0:T(2,128)(2,1)S(1)} %constant_dynamic-slice_fusion.2), kind=kOutput, calls=%fused_computation.104.clone.1 | convolution fusion | flops 545261568 | bytes 10227712 | tf_op jit(solution)/shard_map/while/body/eval_jaxpr/sub | solution.py:19
  75.5 4.7 fusion.88
  80.2 1.0 copy_dynamic-update-slice_fusion.2
  83.7 0.6 iota_add_fusion.2
  84.5 1.1 constant_dynamic-slice_fusion.2
  85.6 2.0 fusion.86
  87.6 7.8 %fusion.87 = (f32[2,512]{1,0:T(2,128)S(1)}, f32[2,512,2048]{2,1,0:T(8,128)}) fusion(pred[512,2048]{1,0:T(8,128)(4,1)} %fusion.86, bf16[2048,128]{1,0:T(8,128)(2,1)} %get-tuple-element.235, bf16[1,512,2,128]{3,2,1,0:T(2,128)(2,1)S(1)} %constant_dynamic-slice_fusion.2), kind=kOutput, calls=%fused_computation.104.clone.1 | convolution fusion | flops 545261568 | bytes 10227712 | tf_op jit(solution)/shard_map/while/body/eval_jaxpr/sub | solution.py:19
  95.4 4.7 fusion.88
  100.1 1.0 copy_dynamic-update-slice_fusion.2
  103.6 0.6 iota_add_fusion.2
  104.4 1.1 constant_dynamic-slice_fusion.2
  105.5 2.0 fusion.86
  107.5 7.8 %fusion.87 = (f32[2,512]{1,0:T(2,128)S(1)}, f32[2,512,2048]{2,1,0:T(8,128)}) fusion(pred[512,2048]{1,0:T(8,128)(4,1)} %fusion.86, bf16[2048,128]{1,0:T(8,128)(2,1)} %get-tuple-element.235, bf16[1,512,2,128]{3,2,1,0:T(2,128)(2,1)S(1)} %constant_dynamic-slice_fusion.2), kind=kOutput, calls=%fused_computation.104.clone.1 | convolution fusion | flops 545261568 | bytes 10227712 | tf_op jit(solution)/shard_map/while/body/eval_jaxpr/sub | solution.py:19
  115.3 4.7 fusion.88
  120.0 1.0 copy_dynamic-update-slice_fusion.2
  123.5 0.6 iota_add_fusion.2
  124.3 1.1 constant_dynamic-slice_fusion.2
  125.4 2.0 fusion.86
  127.4 7.8 %fusion.87 = (f32[2,512]{1,0:T(2,128)S(1)}, f32[2,512,2048]{2,1,0:T(8,128)}) fusion(pred[512,2048]{1,0:T(8,128)(4,1)} %fusion.86, bf16[2048,128]{1,0:T(8,128)(2,1)} %get-tuple-element.235, bf16[1,512,2,128]{3,2,1,0:T(2,128)(2,1)S(1)} %constant_dynamic-slice_fusion.2), kind=kOutput, calls=%fused_computation.104.clone.1 | convolution fusion | flops 545261568 | bytes 10227712 | tf_op jit(solution)/shard_map/while/body/eval_jaxpr/sub | solution.py:19
  135.2 4.7 fusion.88
  139.9 1.0 copy_dynamic-update-slice_fusion.2
  140.9 9.7 %convolution_convert_fusion = bf16[2048,3072]{1,0:T(8,128)(2,1)} fusion(bf16[256,3072]{1,0:T(8,128)(2,1)} %param.20, bf16[256,8,2,128]{3,2,1,0:T(2,128)(2,1)} %bitcast.146), kind=kOutput, calls=%fused_computation.27 | convolution fusion | flops 3227516928 | bytes 15204352 | tf_op jit(solution)/shard_map/dot_general | solution.py:97
  153.0 90.0 %reduce-scatter.2.cloned.1.call-done = bf16[128,3072]{1,0:T(8,128)(2,1)} async-done(((bf16[2048,3072]{1,0:T(8,128)(2,1)}), bf16[128,3072]{1,0:T(8,128)(2,1)}) %reduce-scatter.2.cloned.1.call-update) | async-done | bytes 786448 | tf_op jit(solution)/shard_map/reduce_scatter | solution.py:96
  243.0 1.7 multiply_reduce_fusion
  244.7 1.7 multiply_convert_fusion.1
  246.4 0.9 copy-done.2
  247.3 1.8 convolution_convert_fusion.1
  249.1 2.7 reshape.387
  251.8 30.4 %all_to_all.45 = bf16[8,34,3072]{2,1,0:T(8,128)(2,1)} all-to-all(bf16[8,34,3072]{2,1,0:T(8,128)(2,1)} %reshape.387), channel_id=1, replica_groups=mesh['seq'=16,'exp'=8] {'exp'}, dimensions={0} | all-to-all | bytes 3342336 | tf_op jit(solution)/shard_map/all_to_all | solution.py:147
  282.2 2.6 reshape.388
  285.5 1.9 select_reduce_fusion.3
  288.9 3.3 all-to-all-start.2
  292.3 2.6 fusion.30
  295.0 0.8 mul.166
  295.8 1.6 all-to-all-done.2
  297.5 22.4 %all-gather = bf16[16,272,2]{1,2,0:T(2,128)(2,1)S(1)} all-gather(bf16[1,272,2]{1,2,0:T(2,128)(2,1)S(1)} %reshape.401), channel_id=1, replica_groups=mesh['seq'=16,'exp'=8] {'seq'}, dimensions={0}, use_global_device_ids=true | all-gather | bytes 18496 | tf_op jit(solution)/shard_map/all_gather | solution.py:154
  320.0 0.8 broadcast_multiply_fusion
  320.8 1.1 mul.183
  321.9 122.7 %all-gather.3.cloned.1.call-done = bf16[4352,3072]{1,0:T(8,128)(2,1)} async-done(((bf16[272,3072]{1,0:T(8,128)(2,1)}), bf16[4352,3072]{1,0:T(8,128)(2,1)}) %all-gather.3.cloned.1.call-update) | async-done | bytes 26738704 | tf_op jit(solution)/shard_map/all_gather | solution.py:153
  444.6 19.5 %fusion.28 = f32[4352,512]{1,0:T(8,128)} fusion(bf16[4352,3072]{1,0:T(8,128)(2,1)} %all-gather.3.cloned.1.call-done, bf16[1,3072,512]{2,1,0:T(8,128)(2,1)S(1)} %copy-done), kind=kOutput, calls=%fused_computation.34 | convolution fusion | flops 13690208256 | bytes 38797312 | tf_op jit(solution)/shard_map/dot_general | solution.py:27
  464.2 24.4 %convolution_multiply_fusion = f32[4352,512]{1,0:T(8,128)} fusion(bf16[4352,3072]{1,0:T(8,128)(2,1)} %all-gather.3.cloned.1.call-done, f32[4352,512]{1,0:T(8,128)} %fusion.28, bf16[1,3072,512]{2,1,0:T(8,128)(2,1)} %param.24), kind=kOutput, calls=%fused_computation.28 | convolution fusion | flops 13701349376 | bytes 47710208 | tf_op jit(solution)/shard_map/dot_general | solution.py:28
  488.6 6.2 fusion.59
  494.8 2.0 convolution_add_fusion
  496.9 142.6 %all-reduce.2.cloned.1.call-done = f32[16,3072]{1,0:T(8,128)} async-done(((f32[16,3072]{1,0:T(8,128)}), f32[16,3072]{1,0:T(8,128)}) %all-reduce.2.cloned.1.call-update) | async-done | bytes 196624 | tf_op jit(solution)/shard_map/psum | solution.py:166
  639.4 1.2 convolution_bitcast_fusion
  641.8 2.4 multiply_convert_fusion
  644.8 1.8 fusion.60
  (91 shorter events, 9.2 us)
Async XLA Ops:
  7.2 437.5 %copy-start = (bf16[1,3072,512]{2,1,0:T(8,128)(2,1)S(1)}, bf16[1,3072,512]{2,1,0:T(8,128)(2,1)}, u32[]{:S(2)}) copy-start(bf16[1,3072,512]{2,1,0:T(8,128)(2,1)} %param.23) | copy-start | bytes 9437188
  13.0 30.3 %copy-start.10 = (s32[1,2]{1,0:T(1,128)S(1)}, s32[1,2]{1,0:T(1,128)}, u32[]{:S(2)}) copy-start(s32[1,2]{1,0:T(1,128)} %param.27) | copy-start | bytes 28
  13.0 25.8 %all-to-all-start.1 = ((bf16[128,16,256]{0,2,1:T(8,128)(2,1)}), bf16[128,16,256]{0,2,1:T(8,128)(2,1)}, u32[]{:S(2)}, u32[]{:S(2)}) async-start(bf16[128,16,256]{0,2,1:T(8,128)(2,1)} %bitcast.140), calls=%async_computation.1 | async-start | bytes 2097152 | tf_op jit(solution)/shard_map/all_to_all | solution.py:72
  38.8 20.2 %all-to-all-start = ((bf16[128,16,256]{2,0,1:T(8,128)(2,1)}), bf16[128,16,256]{2,0,1:T(8,128)(2,1)}, u32[]{:S(2)}, u32[]{:S(2)}) async-start(bf16[128,16,256]{2,0,1:T(8,128)(2,1)} %copy.101), calls=%async_computation | async-start | bytes 2097152 | tf_op jit(solution)/shard_map/all_to_all | solution.py:71
  43.2 199.8 %reduce-scatter.2.cloned.1.call-start = ((), (), s32[]{:S(2)}) async-start(), calls=%async_computation.5 | async-start | bytes 13369344 | tf_op jit(solution)/shard_map/reduce_scatter | solution.py:96
  150.7 0.7 copy-start.9
  150.7 94.1 %copy-start.6 = (f32[3072]{0:T(1024)S(1)}, f32[3072]{0:T(1024)}, u32[]{:S(2)}) copy-start(f32[3072]{0:T(1024)} %param.21) | copy-start | bytes 36868
  150.7 293.9 %all-gather.3.cloned.1.call-start = ((), (), s32[]{:S(2)}) async-start(), calls=%async_computation.6 | async-start | bytes 28409856 | tf_op jit(solution)/shard_map/all_gather | solution.py:153
  246.4 0.9 copy-start.2
  288.9 8.4 %all-to-all-start.2 = ((bf16[8,34,2]{1,2,0:T(2,128)(2,1)}), bf16[8,34,2]{1,2,0:T(2,128)(2,1)S(1)}, u32[]{:S(2)}, u32[]{:S(2)}) async-start(bf16[8,34,2]{1,2,0:T(2,128)(2,1)} %copy.113), calls=%async_computation.3 | async-start | bytes 8192 | tf_op jit(solution)/shard_map/all_to_all | solution.py:148
  292.3 347.2 %all-reduce.2.cloned.1.call-start = ((), (), s32[]{:S(2)}) async-start(), calls=%async_computation.7 | async-start | bytes 393216 | tf_op jit(solution)/shard_map/psum | solution.py:166
  488.6 6.2 copy-start.3
  488.6 6.2 copy-start.4
  488.6 8.3 %copy-start.8 = (s32[8,4,2]{0,2,1:T(2,128)S(1)}, s32[8,4,2]{0,2,1:T(2,128)}, u32[]{:S(2)}) copy-start(s32[8,4,2]{0,2,1:T(2,128)} %param.29) | copy-start | bytes 772
  488.6 150.8 %copy-start.5 = (f32[3072]{0:T(1024)S(1)}, f32[3072]{0:T(1024)}, u32[]{:S(2)}) copy-start(f32[3072]{0:T(1024)} %param.26) | copy-start | bytes 36868
  488.6 158.0 %copy-start.1 = (bf16[1,3072,512]{2,1,0:T(8,128)(2,1)S(1)}, bf16[1,3072,512]{2,1,0:T(8,128)(2,1)}, u32[]{:S(2)}) copy-start(bf16[1,3072,512]{2,1,0:T(8,128)(2,1)} %param.23) | copy-start | bytes 9437188
  640.8 5.8 copy-start.7
Sparse Core Ops, SparseCore 0:
  150.8 92.1 reduce-scatter.1
  285.0 159.6 all-gather.2
  497.0 142.4 all-reduce.1
where the time goes:
time: 656 us; the launch traced here: 654 us
  waiting for transfers between devices  383 us (58%)
  matrix products  122 us (19%)
  blocking collectives  52.8 us (8%)
  local copies, waits for them, and re-layouts  36.9 us (6%)
  other arithmetic  20.1 us (3%)
  starting transfers between devices  16.1 us (2%)
  between operations  15.9 us (2%)
  loops' own time  7.85 us (1%)
    psum x1, waiting for transfers between devices, per_device(): pooled = lax.psum(pooled_part, ('seq', 'exp'))  143 us
    all_gather x1, waiting for transfers between devices, per_device(): lax.all_gather(flat_rows, 'seq', axis=0, tiled=True)  123 us
    reduce_scatter x1, waiting for transfers between devices, per_device(): lax.psum_scatter(jnp.dot(attended, out_proj, preferred_element_type=jnp.f...  90 us
    sub x4, matrix products, softmax_block(): exponent = jnp.exp(scores - largest)  31.2 us
    all_to_all x1, blocking collectives, per_device(): lax.all_to_all(slot_rows, 'exp', split_axis=0, concat_axis=0, tiled=True)  30.4 us
    dot_general x1, matrix products, expert_terms(): up_vals = jnp.dot(row_block, up_cols, preferred_element_type=jnp.float32)  24.4 us
    all_gather x1, blocking collectives, per_device(): lax.all_gather(flat_share, 'seq', axis=0, tiled=True)  22.4 us
    dot_general x1, matrix products, expert_terms(): jnp.dot(row_block, gate_cols, preferred_element_type=jnp.float32)  19.5 us
  transfers between devices with their start and end apart: 6, of which 6 were waited for; matrix products, arithmetic and copies ran while one was open for 3% of the time, Pallas kernels for 0%

commit v1 on v0

v1 whole, which is shorter than its diff:
```python
import functools

import jax
import jax.numpy as jnp
from jax import lax
from jax.experimental import pallas as pl
from jax.experimental.pallas import tpu as pltpu
from jax.sharding import PartitionSpec as P

D = 3072
HALF = D // 2
EXT = 128
WIDE = D + EXT
Q_HEADS = 32
KV_HEADS = 8
HEAD_DIM = 128
SEQS = 2
TOK = 128
EXPERTS = 8
CAP = 34
ROWS = EXPERTS * CAP
MAIN = 32
REST = ROWS - EXPERTS * MAIN
NEG = -1e30
F32 = jnp.float32
BF16 = jnp.bfloat16
MESH = pl.DeviceIdType.MESH
VMEM_LIMIT = 60 * 1024 * 1024


def place():
    s = lax.axis_index("seq")
    e = lax.axis_index("exp")
    return s // 4, s % 4, e


def greet(devices):
    barrier = pltpu.get_barrier_semaphore()
    for device in devices:
        pl.semaphore_signal(barrier, inc=1, device_id=device, device_id_type=MESH)
    pl.semaphore_wait(barrier, len(devices))


def remote(src, dst, send, recv, device):
    return pltpu.make_async_remote_copy(
        src_ref=src, dst_ref=dst, send_sem=send, recv_sem=recv, device_id=device, device_id_type=MESH
    )


def lhs_t(a, b):
    return lax.dot_general(a, b, (((0,), (0,)), ((), ())), preferred_element_type=F32)


def rhs_t(a, b):
    return lax.dot_general(a, b, (((1,), (1,)), ((), ())), preferred_element_type=F32)


def mm(a, b):
    return jnp.dot(a, b, preferred_element_type=F32)


def attn_kernel(len_ref, q_ref, k_ref, v_ref, o_ref, qb, kb, vb, lsem, zs, zr, xs, xr):
    z, x, e = place()
    at = lambda zz, xx: (zz * 4 + xx, e)
    greet([at((z + d) % 4, x) for d in (1, 2, 3)] + [at(z, (x + 1) % 4), at(z, (x + 3) % 4)])
    mine = pl.ds(pl.multiple_of(x * TOK, TOK), TOK)
    cols_k = lambda zz: pl.ds(pl.multiple_of(zz * 256, 256), 256)
    cols_q = lambda zz: pl.ds(pl.multiple_of(zz * 1024, 1024), 1024)

    kv_z, q_z = [], []
    for d in (1, 2, 3):
        zt = (z + d) % 4
        to = at(zt, x)
        kv_z.append(
            (
                remote(k_ref.at[:, cols_k(zt)], kb.at[z, mine], zs.at[0, d - 1], zr.at[0, d - 1], to),
                remote(v_ref.at[:, cols_k(zt)], vb.at[z, mine], zs.at[1, d - 1], zr.at[1, d - 1], to),
            )
        )
        q_z.append(remote(q_ref.at[:, cols_q(zt)], qb.at[z], zs.at[2, d - 1], zr.at[2, d - 1], to))
    for d in (2, 1, 3):
        for copy in kv_z[d - 1]:
            copy.start()
    local = [
        pltpu.make_async_copy(k_ref.at[:, cols_k(z)], kb.at[z, mine], lsem.at[0]),
        pltpu.make_async_copy(v_ref.at[:, cols_k(z)], vb.at[z, mine], lsem.at[1]),
        pltpu.make_async_copy(q_ref.at[:, cols_q(z)], qb.at[z], lsem.at[2]),
    ]
    for copy in local:
        copy.start()
    for d in (2, 1, 3):
        q_z[d - 1].start()
    local[0].wait()
    local[1].wait()

    plus, minus = (x + 1) % 4, (x + 3) % 4
    rows = lambda xx: pl.ds(pl.multiple_of(xx * TOK, TOK), TOK)
    near, far = [], []
    for d in (0, 1, 2, 3):
        zz = (z + 4 - d) % 4
        near.append(
            [
                remote(kb.at[zz, mine], kb.at[zz, mine], xs.at[0, d], xr.at[0, d], at(z, plus)),
                remote(vb.at[zz, mine], vb.at[zz, mine], xs.at[1, d], xr.at[1, d], at(z, plus)),
                remote(kb.at[zz, mine], kb.at[zz, mine], xs.at[2, d], xr.at[2, d], at(z, minus)),
                remote(vb.at[zz, mine], vb.at[zz, mine], xs.at[3, d], xr.at[3, d], at(z, minus)),
            ]
        )
        left, right = rows(minus), rows(plus)
        far.append(
            [
                remote(kb.at[zz, left], kb.at[zz, left], xs.at[4, d], xr.at[4, d], at(z, plus)),
                remote(vb.at[zz, right], vb.at[zz, right], xs.at[5, d], xr.at[5, d], at(z, minus)),
            ]
        )
    order = (0, 1, 3, 2)
    for d in order:
        if d:
            kv_z[d - 1][0].wait_recv()
            kv_z[d - 1][1].wait_recv()
        for copy in near[d]:
            copy.start()
    for d in order:
        near[d][0].wait_recv()
        far[d][0].start()
        near[d][3].wait_recv()
        far[d][1].start()
    local[2].wait()
    for d in (1, 3, 2):
        q_z[d - 1].wait_recv()
    for d in order:
        near[d][1].wait_recv()
        near[d][2].wait_recv()
        far[d][0].wait_recv()
        far[d][1].wait_recv()

    bound = len_ref[0, 0]
    scale = HEAD_DIM ** (-0.5) * 1.4426950408889634

    def query_step(zq, _):
        q_all = qb[zq]
        stacked = [
            jnp.concatenate(
                [q_all[:, (4 * h + j) * 128 : (4 * h + j + 1) * 128] for j in range(4)], axis=0
            )
            for h in range(2)
        ]
        qpos = (zq * 4 + x) * TOK + lax.broadcasted_iota(jnp.int32, (TOK, 512), 0)
        first = jnp.where(qpos >= bound, bound, 0)

        def key_step(kz, carry):
            kpos = kz * 512 + lax.broadcasted_iota(jnp.int32, (TOK, 512), 1)
            bias = jnp.where(jnp.logical_and(kpos <= qpos, kpos >= first), 0.0, NEG)
            out = []
            for h in range(2):
                m, l, acc = carry[h]
                sc = rhs_t(stacked[h], kb[kz, :, h * 128 : (h + 1) * 128])
                sc = (sc.reshape(4, TOK, 512) + bias[None]).reshape(512, 512)
                mn = jnp.maximum(m, jnp.max(sc, axis=1, keepdims=True))
                p = jnp.exp2((sc - mn) * scale)
                a = jnp.exp2((m - mn) * scale)
                l = a * l + jnp.sum(p, axis=1, keepdims=True)
                acc = a * acc + mm(p.astype(BF16), vb[kz, :, h * 128 : (h + 1) * 128])
                out.append((mn, l, acc))
            return tuple(out)

        start = (
            jnp.full((512, 1), NEG, F32),
            jnp.zeros((512, 1), F32),
            jnp.zeros((512, 128), F32),
        )
        done = lax.fori_loop(0, zq + 1, key_step, (start, start))
        for h in range(2):
            _, l, acc = done[h]
            res = (acc / l).astype(BF16)
            for j in range(4):
                o_ref[zq, :, (4 * h + j) * 128 : (4 * h + j + 1) * 128] = res[j * 128 : (j + 1) * 128]
        return 0

    lax.fori_loop(0, 4, query_step, 0)
    for d in range(3):
        kv_z[d][0].wait_send()
        kv_z[d][1].wait_send()
        q_z[d].wait_send()
    for d in range(4):
        for copy in near[d] + far[d]:
            copy.wait_send()


def attention(lengths, q, k, v):
    any_spec = pl.BlockSpec(memory_space=pl.ANY)
    return pl.pallas_call(
        attn_kernel,
        out_shape=jax.ShapeDtypeStruct((4, TOK, 1024), BF16),
        in_specs=[pl.BlockSpec(memory_space=pltpu.SMEM), any_spec, any_spec, any_spec],
        out_specs=pl.BlockSpec(memory_space=pltpu.VMEM),
        scratch_shapes=[
            pltpu.VMEM((4, TOK, 1024), BF16),
            pltpu.VMEM((4, 512, 256), BF16),
            pltpu.VMEM((4, 512, 256), BF16),
            pltpu.SemaphoreType.DMA((3,)),
            pltpu.SemaphoreType.DMA((3, 3)),
            pltpu.SemaphoreType.DMA((3, 3)),
            pltpu.SemaphoreType.DMA((6, 4)),
            pltpu.SemaphoreType.DMA((6, 4)),
        ],
        compiler_params=pltpu.CompilerParams(
            collective_id=0, has_side_effects=True, vmem_limit_bytes=VMEM_LIMIT
        ),
        cost_estimate=pl.CostEstimate(
            flops=4_000_000_000, bytes_accessed=4_000_000, transcendentals=5_000_000
        ),
        name="attention",
    )(lengths, q, k, v)


def moe_kernel(
    len_ref, att, wz, res, gain, router, routes, wg_hbm, wu_hbm,
    hs_out, pool_out,
    part, rs, hid, nrm, stage, pack, unpack, xb, wg, wu, hs, hr,
    rs_s, rs_r, w_s, w_r, y_s, y_r, z_s, z_r, x_s, x_r, h_s, h_r, lsem,
):
    z, x, e = place()
    core = e % 2
    swap, flip = x + 1 - 2 * (x % 2), 3 - x
    x_weight = swap * (1 - core) + flip * core
    x_token = flip * (1 - core) + swap * core
    at = lambda zz, xx, ee: (zz * 4 + xx, ee)
    zp, zm = at((z + 1) % 4, x, e), at((z + 3) % 4, x, e)
    partner_w, partner_t = at(z, x_weight, e), at(z, x_token, e)
    greet([at(z, x, (e + d) % 8) for d in range(1, 8)] + [zp, zm, partner_w, partner_t])

    own_w, far_w = [], []
    for c in range(2):
        cols = pl.ds(c * 256, 256)
        for i, (hbm, buf) in enumerate(((wg_hbm, wg), (wu_hbm, wu))):
            own_w.append(pltpu.make_async_copy(hbm.at[:, cols], buf.at[c], lsem.at[2 * c + i]))
            far_w.append(
                remote(hbm.at[:, cols], buf.at[2 + c], w_s.at[2 * c + i], w_r.at[2 * c + i], partner_w)
            )

    def project(target, half):
        return mm(att[target], wz[:, half * HALF : (half + 1) * HALF])

    z2, z1, z3 = (z + 2) % 4, (z + 1) % 4, (z + 3) % 4
    rsc = [
        remote(part.at[i], rs.at[i], rs_s.at[i], rs_r.at[i], zp if i % 2 == 0 else zm)
        for i in range(6)
    ]
    part[0] = project(z2, 0).astype(BF16)
    rsc[0].start()
    part[1] = project(z2, 1).astype(BF16)
    rsc[1].start()
    for copy in own_w + far_w:
        copy.start()
    part[2] = project(z1, 1).astype(BF16)
    rsc[2].start()
    part[3] = project(z3, 0).astype(BF16)
    rsc[3].start()
    through_a = project(z1, 0)
    rsc[0].wait_recv()
    part[4] = (through_a + rs[0].astype(F32)).astype(BF16)
    rsc[4].start()
    through_b = project(z3, 1)
    rsc[1].wait_recv()
    part[5] = (through_b + rs[1].astype(F32)).astype(BF16)
    rsc[5].start()
    for half in range(2):
        span = slice(half * HALF, (half + 1) * HALF)
        hid[:, span] = res[:, span].astype(F32) + project(z, half)

    ids = lax.broadcasted_iota(jnp.int32, (TOK, EXPERTS), 1)
    hot = [ids == routes[:, k : k + 1] for k in range(2)]
    named = jnp.where(jnp.logical_or(hot[0], hot[1]), 1.0, 0.0).astype(BF16)
    earlier = jnp.where(
        lax.broadcasted_iota(jnp.int32, (TOK, TOK), 1) < lax.broadcasted_iota(jnp.int32, (TOK, TOK), 0),
        1.0,
        0.0,
    ).astype(BF16)
    before = mm(earlier, named)
    slot_ids = lax.broadcasted_iota(jnp.int32, (TOK, ROWS), 1)
    slot_hot = []
    for k in range(2):
        rank = jnp.sum(jnp.where(hot[k], before, 0.0), axis=1, keepdims=True).astype(jnp.int32)
        expert = routes[:, k : k + 1]
        slot = jnp.where(
            rank < MAIN, expert * MAIN + rank, EXPERTS * MAIN + expert * 2 + (rank - MAIN)
        )
        slot_hot.append(jnp.where(slot_ids == slot, 1.0, 0.0).astype(BF16))
    slot_any = slot_hot[0] + slot_hot[1]
    bound = len_ref[0, 0]
    second = len_ref[0, 1]
    tpos = (z * 4 + x) * TOK + lax.broadcasted_iota(jnp.int32, (TOK, 1), 0)
    in_second = tpos >= bound
    own_len = jnp.where(in_second, second, bound).astype(F32)

    rsc[2].wait_recv()
    rsc[3].wait_recv()
    hid[:, :HALF] = hid[:, :HALF] + rs[3].astype(F32)
    hid[:, HALF:] = hid[:, HALF:] + rs[2].astype(F32)
    rsc[4].wait_recv()
    rsc[5].wait_recv()
    hid[:, :HALF] = hid[:, :HALF] + rs[4].astype(F32)
    hid[:, HALF:] = hid[:, HALF:] + rs[5].astype(F32)

    square = jnp.sum(hid[...] * hid[...], axis=1, keepdims=True) * (1.0 / D)
    norm_scale = lax.rsqrt(square + 1e-05)
    nrm[...] = (hid[...] * norm_scale * gain[...]).astype(BF16)

    r_all = router[...]
    r_hi = r_all.astype(BF16)
    r_rest = r_all - r_hi.astype(F32)
    r_mid = r_rest.astype(BF16)
    r_low = (r_rest - r_mid.astype(F32)).astype(BF16)
    logits = rhs_t(nrm[...], r_hi) + rhs_t(nrm[...], r_mid) + rhs_t(nrm[...], r_low)
    picked = [jnp.sum(jnp.where(hot[k], logits, 0.0), axis=1, keepdims=True) for k in range(2)]
    gates = [
        1.0 / (1.0 + jnp.exp(picked[1] - picked[0])),
        1.0 / (1.0 + jnp.exp(picked[0] - picked[1])),
    ]
    bucket = jnp.where(in_second, 8, 0) + e
    lanes = lax.broadcasted_iota(jnp.int32, (TOK, EXT), 1)
    ext = jnp.zeros((ROWS, EXT), F32)
    for k in range(2):
        weight = (gates[k] / own_len).astype(BF16).astype(F32)
        ext = ext + lhs_t(slot_hot[k], jnp.where(lanes == bucket, weight, 0.0).astype(BF16))
    for c in range(4):
        span = slice(c * 768, (c + 1) * 768)
        stage[:, span] = lhs_t(slot_any, nrm[:, span]).astype(BF16)
    stage[:, D:] = ext.astype(BF16)

    tall = lax.broadcasted_iota(jnp.int32, (TOK, REST), 0)
    wide = lax.broadcasted_iota(jnp.int32, (TOK, REST), 1)
    base = (wide // 2) * 16 + (wide % 2) * 8
    for j in range(4):
        got = jnp.zeros((TOK, 128), F32)
        for kk in range(8):
            chunk = 8 * j + kk
            if chunk * 128 < WIDE:
                pick = jnp.where(tall == base + kk, 1.0, 0.0).astype(BF16)
                got = got + mm(pick, stage[EXPERTS * MAIN :, chunk * 128 : (chunk + 1) * 128])
        pack[:, :, j * 128 : (j + 1) * 128] = got.astype(BF16).reshape(EXPERTS, 16, 128)

    own_slot = 2 * z
    my_rows = pl.ds(pl.multiple_of(e * MAIN, MAIN), MAIN)
    y_copies = []
    for d in range(1, 8):
        et = (e + d) % 8
        to = at(z, x, et)
        y_copies.append(
            remote(
                stage.at[pl.ds(pl.multiple_of(et * MAIN, MAIN), MAIN)],
                xb.at[own_slot, my_rows],
                y_s.at[0, d - 1],
                y_r.at[0, d - 1],
                to,
            )
        )
        y_copies.append(remote(pack.at[et], unpack.at[e], y_s.at[1, d - 1], y_r.at[1, d - 1], to))
    for copy in y_copies:
        copy.start()
    keep = [
        pltpu.make_async_copy(stage.at[my_rows], xb.at[own_slot, my_rows], lsem.at[4]),
        pltpu.make_async_copy(pack.at[e], unpack.at[e], lsem.at[5]),
    ]
    for copy in keep:
        copy.start()

    inv = 1.0 / own_len
    pool_out[...] = jnp.zeros_like(pool_out)
    pool_out[0:1] = jnp.sum(hid[...] * jnp.where(in_second, 0.0, inv), axis=0, keepdims=True)
    pool_out[1:2] = jnp.sum(hid[...] * jnp.where(in_second, inv, 0.0), axis=0, keepdims=True)
    hs[...] = jnp.zeros_like(hs)

    for copy in keep:
        copy.wait()
    for copy in y_copies:
        copy.wait_recv()
    flat = unpack[...].reshape(TOK, 512)
    tall_t = lax.broadcasted_iota(jnp.int32, (REST, TOK), 0)
    wide_t = lax.broadcasted_iota(jnp.int32, (REST, TOK), 1)
    base_t = (tall_t // 2) * 16 + (tall_t % 2) * 8
    for kk in range(8):
        pick = jnp.where(wide_t == base_t + kk, 1.0, 0.0).astype(BF16)
        got = mm(pick, flat).astype(BF16)
        for j in range(4):
            chunk = 8 * j + kk
            if chunk * 128 < WIDE:
                xb[own_slot, EXPERTS * MAIN :, chunk * 128 : (chunk + 1) * 128] = got[
                    :, j * 128 : (j + 1) * 128
                ]

    slot_of = lambda d: 2 * ((z + 4 - d) % 4)
    top, bottom = pl.ds(0, 128), pl.ds(128, ROWS - 128)
    zc = [
        remote(xb.at[own_slot], xb.at[own_slot], z_s.at[0], z_r.at[0], zp),
        remote(xb.at[own_slot], xb.at[own_slot], z_s.at[1], z_r.at[1], zm),
        remote(xb.at[slot_of(1), top], xb.at[slot_of(1), top], z_s.at[2], z_r.at[2], zp),
        remote(xb.at[slot_of(3), bottom], xb.at[slot_of(3), bottom], z_s.at[3], z_r.at[3], zm),
    ]
    xc = [
        remote(xb.at[slot_of(d)], xb.at[slot_of(d) + 1], x_s.at[d], x_r.at[d], partner_t)
        for d in range(4)
    ]
    zc[0].start()
    zc[1].start()
    xc[0].start()

    for copy in own_w + far_w[:0]:
        copy.wait()

    def experts(slot):
        def chunk_step(c, _):
            rows = xb[slot, :, :D]
            gate = mm(rows, wg[c])
            up = mm(rows, wu[c])
            act = (gate / (1.0 + jnp.exp(-gate)) * up).astype(BF16)
            hs[c] = hs[c] + lhs_t(xb[slot, :, D:], act)
            return 0

        lax.fori_loop(0, 4, chunk_step, 0)

    zc[0].wait_recv()
    zc[2].start()
    xc[1].start()
    zc[1].wait_recv()
    zc[3].start()
    xc[3].start()
    for copy in far_w:
        copy.wait_recv()
    experts(own_slot)
    experts(slot_of(1))
    zc[2].wait_recv()
    zc[3].wait_recv()
    xc[2].start()
    experts(slot_of(3))
    xc[0].wait_recv()
    experts(own_slot + 1)
    experts(slot_of(2))
    for d in (1, 3, 2):
        xc[d].wait_recv()
        experts(slot_of(d) + 1)

    home = remote(hs.at[pl.ds(2, 2), pl.ds(0, 16)], hr, h_s, h_r, partner_w)
    home.start()
    home.wait_recv()
    for c in range(2):
        hs_out[:, c * 256 : (c + 1) * 256] = hs[c, 0:16] + hr[c]
    home.wait_send()
    for copy in rsc + far_w + y_copies + zc + xc:
        copy.wait_send()


def moe(lengths, att, wz, res, gain, router_t, routes, w_gate, w_up):
    vmem = pl.BlockSpec(memory_space=pltpu.VMEM)
    hbm = pl.BlockSpec(memory_space=pl.ANY)
    dma = pltpu.SemaphoreType.DMA
    return pl.pallas_call(
        moe_kernel,
        out_shape=(
            jax.ShapeDtypeStruct((16, 512), F32),
            jax.ShapeDtypeStruct((8, D), F32),
        ),
        in_specs=[pl.BlockSpec(memory_space=pltpu.SMEM)] + [vmem] * 6 + [hbm, hbm],
        out_specs=(vmem, vmem),
        scratch_shapes=[
            pltpu.VMEM((6, TOK, HALF), BF16),
            pltpu.VMEM((6, TOK, HALF), BF16),
            pltpu.VMEM((TOK, D), F32),
            pltpu.VMEM((TOK, D), BF16),
            pltpu.VMEM((ROWS, WIDE), BF16),
            pltpu.VMEM((EXPERTS, 16, 512), BF16),
            pltpu.VMEM((EXPERTS, 16, 512), BF16),
            pltpu.VMEM((8, ROWS, WIDE), BF16),
            pltpu.VMEM((4, D, 256), BF16),
            pltpu.VMEM((4, D, 256), BF16),
            pltpu.VMEM((4, EXT, 256), F32),
            pltpu.VMEM((2, 16, 256), F32),
            dma((6,)), dma((6,)),
            dma((4,)), dma((4,)),
            dma((2, 7)), dma((2, 7)),
            dma((4,)), dma((4,)),
            dma((4,)), dma((4,)),
            dma, dma,
            dma((6,)),
        ],
        compiler_params=pltpu.CompilerParams(
            collective_id=1, has_side_effects=True, vmem_limit_bytes=VMEM_LIMIT
        ),
        cost_estimate=pl.CostEstimate(
            flops=32_000_000_000, bytes_accessed=20_000_000, transcendentals=3_000_000
        ),
        name="experts",
    )(lengths, att, wz, res, gain, router_t, routes, w_gate, w_up)


def final_kernel(
    hs, pool, vec, head, wd, chosen, rejected,
    rew_out, loss_out, gh_out, wt_out,
    r_mine, r_exp, r_sum, r_seq, g_mine, g_exp, g_sum, g_seq,
    re_s, re_r, rq_s, rq_r, ge_s, ge_r, gq_s, gq_r,
):
    s = lax.axis_index("seq")
    e = lax.axis_index("exp")
    exp_peers = [(s, (e + d) % 8) for d in range(1, 8)]
    seq_peers = [((s + d) % 16, e) for d in range(1, 16)]
    greet(exp_peers + seq_peers)

    def all_sum(mine, got_exp, total, got_seq, es, er, qs, qr):
        copies = [
            remote(mine, got_exp.at[i], es.at[i], er.at[i], to) for i, to in enumerate(exp_peers)
        ]
        for copy in copies:
            copy.start()
        acc = mine[...]
        for i, copy in enumerate(copies):
            copy.wait_recv()
            acc = acc + got_exp[i]
        total[...] = acc
        more = [
            remote(total, got_seq.at[i], qs.at[i], qr.at[i], to) for i, to in enumerate(seq_peers)
        ]
        for copy in more:
            copy.start()
        for i, copy in enumerate(more):
            copy.wait_recv()
            acc = acc + got_seq[i]
        return acc, copies + more

    hsv = hs[...]
    part = jnp.sum(hsv * vec[...], axis=1, keepdims=True)
    own = jnp.sum(pool[...] * head[...], axis=1, keepdims=True)
    group = lax.broadcasted_iota(jnp.int32, (8, 128), 0)
    r_mine[0:8] = part[0:8] + jnp.where(group == e, own[0:1], 0.0)
    r_mine[8:16] = part[8:16] + jnp.where(group == e, own[1:2], 0.0)
    rewards, sent = all_sum(r_mine, r_exp, r_sum, r_seq, re_s, re_r, rq_s, rq_r)
    rew_out[...] = rewards

    r0, r1 = rewards[0:8], rewards[8:16]
    ch, rj = chosen[...], rejected[...]
    margin = jnp.where(ch == 0, r0, r1) - jnp.where(rj == 0, r0, r1)
    real = lax.broadcasted_iota(jnp.int32, (8, 128), 1) < 4
    loss = jnp.maximum(-margin, 0.0) + jnp.log1p(jnp.exp(-jnp.abs(margin)))
    loss = jnp.sum(jnp.where(real, loss, 0.0), axis=1, keepdims=True)
    loss = jnp.sum(loss, axis=0, keepdims=True) * (1.0 / 32.0)
    loss_out[...] = jnp.broadcast_to(loss, (8, 128))
    factor = jnp.where(real, -1.0 / (1.0 + jnp.exp(margin)) * (1.0 / 32.0), 0.0)
    up0 = jnp.where(ch == 0, factor, 0.0) - jnp.where(rj == 0, factor, 0.0)
    up1 = jnp.where(ch == 1, factor, 0.0) - jnp.where(rj == 1, factor, 0.0)
    rg0 = jnp.sum(up0, axis=1, keepdims=True)
    rg1 = jnp.sum(up1, axis=1, keepdims=True)
    weighted = jnp.sum(hsv[0:8] * rg0 + hsv[8:16] * rg1, axis=0, keepdims=True)
    wt_out[...] = jnp.broadcast_to(weighted, (8, 512))
    hi = weighted.astype(BF16).astype(F32)
    mid = (weighted - hi).astype(BF16).astype(F32)
    low = weighted - hi - mid
    line = lax.broadcasted_iota(jnp.int32, (16, 512), 0)
    three = jnp.where(line == 0, hi, jnp.where(line == 1, mid, jnp.where(line == 2, low, 0.0)))
    moved = jnp.sum(mm(three.astype(BF16), wd[...]), axis=0, keepdims=True)
    mine = lax.broadcasted_iota(jnp.int32, (8, 1), 0) == e
    own0 = jnp.sum(jnp.where(mine, rg0, 0.0), axis=0, keepdims=True)
    own1 = jnp.sum(jnp.where(mine, rg1, 0.0), axis=0, keepdims=True)
    grad = moved + own0 * pool[0:1] + own1 * pool[1:2]
    for i in range(24):
        g_mine[i : i + 1] = grad[:, i * 128 : (i + 1) * 128]
    total, more = all_sum(g_mine, g_exp, g_sum, g_seq, ge_s, ge_r, gq_s, gq_r)
    gh_out[...] = total
    for copy in sent + more:
        copy.wait_send()


def final(hs, pool, vec, head, wd, chosen, rejected):
    vmem = pl.BlockSpec(memory_space=pltpu.VMEM)
    dma = pltpu.SemaphoreType.DMA
    return pl.pallas_call(
        final_kernel,
        out_shape=(
            jax.ShapeDtypeStruct((16, 128), F32),
            jax.ShapeDtypeStruct((8, 128), F32),
            jax.ShapeDtypeStruct((24, 128), F32),
            jax.ShapeDtypeStruct((8, 512), F32),
        ),
        in_specs=[vmem] * 7,
        out_specs=(vmem,) * 4,
        scratch_shapes=[
            pltpu.VMEM((16, 128), F32), pltpu.VMEM((7, 16, 128), F32),
            pltpu.VMEM((16, 128), F32), pltpu.VMEM((15, 16, 128), F32),
            pltpu.VMEM((24, 128), F32), pltpu.VMEM((7, 24, 128), F32),
            pltpu.VMEM((24, 128), F32), pltpu.VMEM((15, 24, 128), F32),
            dma((7,)), dma((7,)), dma((15,)), dma((15,)),
            dma((7,)), dma((7,)), dma((15,)), dma((15,)),
        ],
        compiler_params=pltpu.CompilerParams(
            collective_id=2, has_side_effects=True, vmem_limit_bytes=VMEM_LIMIT
        ),
        name="final",
    )(hs, pool, vec, head, wd, chosen, rejected)


def per_device(
    query_states, key_states, value_states, residual, out_proj, norm_gain, router,
    w_gate, w_up, w_down, reward_head, lengths, routes, pair_list,
):
    columns = [[4 * z + x for x in range(4)] for z in range(4)]
    wz = lax.all_gather(out_proj, "seq", axis=0, tiled=True, axis_index_groups=columns)
    att = attention(lengths, query_states[0], key_states[0], value_states[0])
    vec = jnp.sum(w_down[0].astype(F32) * reward_head[None, :], axis=1)[None, :]
    hs, pool = moe(
        lengths, att, wz, residual[0], norm_gain[None, :], router.T, routes[0], w_gate[0], w_up[0]
    )
    pad = ((0, 0), (0, 124))
    rew, loss, gh, wt = final(
        hs, pool, vec, reward_head[None, :], w_down[0],
        jnp.pad(pair_list[:, :, 0], pad), jnp.pad(pair_list[:, :, 1], pad),
    )
    rewards = rew[:, 0].reshape(2, 8).T
    grad_down = (wt[0][:, None] * reward_head[None, :]).astype(BF16)[None]
    return rewards, loss[0, 0], gh.reshape(-1), grad_down


def solution(mesh):
    placed = (
        P("exp", "seq", None), P("exp", "seq", None), P("exp", "seq", None), P("exp", "seq", None),
        P("seq", None), P(), P(), P("exp", None, "seq"), P("exp", None, "seq"),
        P("exp", "seq", None), P(), P("exp", None), P("exp", "seq", None), P(),
    )
    return jax.shard_map(
        per_device,
        mesh=mesh,
        in_specs=placed,
        out_specs=(P(), P(), P(), P("exp", "seq", None)),
        check_vma=False,
    )
```

time: 656 us -> 296 us (0.45)
  waiting for transfers between devices: 383 us -> 15.3 us
  Pallas kernels: 0 us -> 252 us
  matrix products: 122 us -> 0 us
  blocking collectives: 52.8 us -> 0 us
  local copies, waits for them, and re-layouts: 36.9 us -> 8.21 us
  starting transfers between devices: 16.1 us -> 0.04 us
  other arithmetic: 20.1 us -> 5.51 us
  loops' own time: 7.85 us -> 0 us
    pallas_call x0 -> x3, Pallas kernels: none -> 252 us  [the longest x1 163 us: moe(): pl.pallas_call(moe_kernel, out_shape=(jax.ShapeDtypeStruct((16, 512), F32...]
    psum x1 -> x0, waiting for transfers between devices: 143 us -> none  [per_device(): pooled = lax.psum(pooled_part, ('seq', 'exp'))]
    all_gather x1, waiting for transfers between devices: 123 us -> 14.7 us  [per_device(): lax.all_gather(out_proj, 'seq', axis=0, tiled=True, axis_index_groups=col...]
    dot_general x16 -> x0, matrix products: 90.6 us -> none  [the longest x1 24.4 us: expert_terms(): up_vals = jnp.dot(row_block, up_cols, preferred_element_type=jnp.float32)]
    reduce_scatter x1 -> x0, waiting for transfers between devices: 90 us -> none  [per_device(): lax.psum_scatter(jnp.dot(attended, out_proj, preferred_element_type=jnp.f...]
    sub x4 -> x0, matrix products: 31.2 us -> none  [softmax_block(): exponent = jnp.exp(scores - largest)]
    all_to_all x1 -> x0, blocking collectives: 30.4 us -> none  [per_device(): lax.all_to_all(slot_rows, 'exp', split_axis=0, concat_axis=0, tiled=True)]
    all_to_all x3 -> x0, waiting for transfers between devices: 27.4 us -> none  [the longest x1 14.8 us: per_device(): lax.all_to_all(paired, 'seq', split_axis=1, concat_axis=0, tiled=True)]
  transfers between devices with their start and end apart: 6 -> 1, of which waited for: 6 -> 1; matrix products, arithmetic and copies ran while one was open for 3% -> 2% of each run, Pallas kernels for 0% -> 21%
where the time goes in v1:
time: 296 us; the launch traced here: 295 us
  Pallas kernels  252 us (85%)
  waiting for transfers between devices  15.3 us (5%)
  between operations  14.1 us (5%)
  local copies, waits for them, and re-layouts  8.21 us (3%)
  other arithmetic  5.51 us (2%)
    pallas_call x1, Pallas kernels, moe(): pl.pallas_call(moe_kernel, out_shape=(jax.ShapeDtypeStruct((16, 512), F32...  163 us
    pallas_call x1, Pallas kernels, attention(): pl.pallas_call(attn_kernel, out_shape=jax.ShapeDtypeStruct((4, TOK, 1024)...  62.6 us
    pallas_call x1, Pallas kernels, final(): pl.pallas_call(final_kernel, out_shape=(jax.ShapeDtypeStruct((16, 128), F...  26 us
    all_gather x1, waiting for transfers between devices, per_device(): lax.all_gather(out_proj, 'seq', axis=0, tiled=True, axis_index_groups=col...  14.7 us
  transfers between devices with their start and end apart: 1, of which 1 were waited for; matrix products, arithmetic and copies ran while one was open for 2% of the time, Pallas kernels for 21%

profile of v1, /device:TPU:0, one launch (start us, length us, event | category | flops | bytes accessed | tf_op | source)
XLA Modules:
  0.0 295.0 jit_solution(222914616841406472)
XLA Ops:
  7.2 0.0 all-gather.2.cloned.1.call-start
  7.2 0.7 all-gather.2.cloned.1.call-update
  7.9 1.4 copy.21
  9.3 0.8 fusion
  10.1 0.1 copy.22
  10.2 0.1 copy.23
  10.2 0.6 pad.7.chosen
  10.8 0.6 pad.8.rejected
  11.4 3.2 %multiply_reduce_fusion = f32[512]{0:T(512)} fusion(f32[3072]{0:T(1024)} %param.24, bf16[1,512,3072]{2,1,0:T(8,128)(2,1)} %param.23), kind=kLoop, calls=%fused_computation.1 | loop fusion | flops 4718080 | bytes 3160064 | tf_op jit(solution)/shard_map/reduce_sum | solution.py:607
  14.6 62.6 %attention.1.att = bf16[4,128,1024]{2,1,0:T(8,128)(2,1)} custom-call(s32[1,2]{1,0:T(1,128)} %len_ref.3, bf16[128,4096]{1,0:T(8,128)(2,1)} %bitcast.29, bf16[128,1024]{1,0:T(8,128)(2,1)} %bitcast.31, bf16[128,1024]{1,0:T(8,128)(2,1)} %bitcast.32), custom_call_target="tpu_custom_call" | custom-call | flops 4000000000 | bytes 4000000 | tf_op jit(solution)/shard_map/attention/pallas_call | solution.py:192
  77.2 14.7 %all-gather.2.cloned.1.call-done.wz = bf16[1024,3072]{1,0:T(8,128)(2,1)} async-done(((bf16[256,3072]{1,0:T(8,128)(2,1)}), bf16[1024,3072]{1,0:T(8,128)(2,1)}) %all-gather.2.cloned.1.call-update) | async-done | bytes 6291472 | tf_op jit(solution)/shard_map/all_gather | solution.py:605
  91.9 0.0 copy-start
  91.9 163.3 %experts.1 = (f32[16,512]{1,0:T(8,128)}, f32[8,3072]{1,0:T(8,128)}) custom-call(s32[1,2]{1,0:T(1,128)} %len_ref.3, bf16[4,128,1024]{2,1,0:T(8,128)(2,1)} %attention.1.att, bf16[1024,3072]{1,0:T(8,128)(2,1)} %all-gather.2.cloned.1.call-done.wz, bf16[128,3072]{1,0:T(8,128)(2,1)} %bitcast.30, f32[1,3072]{1,0:T(1,128)} %bitcast.34, f32[8,3072]{1,0:T(8,128)} %bitcast.33, ...), custom_call_target="tpu_custom_call" | custom-call | flops 32000000000 | bytes 20000000 | tf_op jit(solution)/shard_map/experts/pallas_call | solution.py:458
  255.2 26.0 %final.1 = (f32[16,128]{1,0:T(8,128)}, f32[8,128]{1,0:T(8,128)}, f32[24,128]{1,0:T(8,128)}, f32[8,512]{1,0:T(8,128)}) custom-call(f32[16,512]{1,0:T(8,128)} %get-tuple-element.10.hs, f32[8,3072]{1,0:T(8,128)} %get-tuple-element.11.pool, f32[1,512]{1,0:T(1,128)} %bitcast.26, f32[1,3072]{1,0:T(1,128)} %bitcast.20, bf16[512,3072]{1,0:T(8,128)(2,1)} %bitcast.19, ...), custom_call_target="tpu_custom_call" | custom-call | tf_op jit(solution)/shard_map/final/pallas_call | solution.py:575
  281.2 0.7 slice.21
  281.9 0.0 copy-done
  281.9 2.3 multiply_convert_fusion
  284.2 0.8 slice_reduce_fusion
  285.0 0.6 reshape_squeeze.3
  285.7 1.2 slice.20
  286.9 1.3 copy.25
Async XLA Ops:
  7.2 84.7 %all-gather.2.cloned.1.call-start = ((), (), s32[]{:S(2)}) async-start(), calls=%async_computation | async-start | bytes 7864320 | tf_op jit(solution)/shard_map/all_gather | solution.py:605
  91.9 190.0 %copy-start = (f32[3072]{0:T(1024)S(1)}, f32[3072]{0:T(1024)}, u32[]{:S(2)}) copy-start(f32[3072]{0:T(1024)} %param.24) | copy-start | bytes 36868
Sparse Core Ops, SparseCore 0:
  9.7 82.1 all-gather.1

commit v2 on v1

v2 whole, which is shorter than its diff:
```python
import functools

import jax
import jax.numpy as jnp
from jax import lax
from jax.experimental import pallas as pl
from jax.experimental.pallas import tpu as pltpu
from jax.sharding import PartitionSpec as P

D = 3072
BLK = 384
CHUNKS = 4
CW = D // CHUNKS
X_FIRST = (1,)
EXT = 128
WIDE = D + EXT
Q_HEADS = 32
KV_HEADS = 8
HEAD_DIM = 128
SEQS = 2
TOK = 128
EXPERTS = 8
CAP = 34
ROWS = EXPERTS * CAP
MAIN = 32
REST = ROWS - EXPERTS * MAIN
NEG = -1e30
F32 = jnp.float32
BF16 = jnp.bfloat16
MESH = pl.DeviceIdType.MESH
VMEM_LIMIT = 60 * 1024 * 1024


def place():
    s = lax.axis_index("seq")
    e = lax.axis_index("exp")
    return s // 4, s % 4, e


def greet(devices):
    barrier = pltpu.get_barrier_semaphore()
    for device in devices:
        pl.semaphore_signal(barrier, inc=1, device_id=device, device_id_type=MESH)
    pl.semaphore_wait(barrier, len(devices))


def remote(src, dst, send, recv, device):
    return pltpu.make_async_remote_copy(
        src_ref=src, dst_ref=dst, send_sem=send, recv_sem=recv, device_id=device, device_id_type=MESH
    )


def lhs_t(a, b):
    return lax.dot_general(a, b, (((0,), (0,)), ((), ())), preferred_element_type=F32)


def rhs_t(a, b):
    return lax.dot_general(a, b, (((1,), (1,)), ((), ())), preferred_element_type=F32)


def mm(a, b):
    return jnp.dot(a, b, preferred_element_type=F32)


def layer_kernel(
    len_ref, q_ref, k_ref, v_ref, op_ref, res, gain, router, routes, wg_hbm, wu_hbm,
    hs_out, pool_out,
    qb, kb, vb, att, wb, part, rs, hid, nrm, stage, pack, unpack, xb, wg, wu, hs, hr,
    lsem, zs, zr, xs, xr, o_s, o_r, rs_s, rs_r, w_s, w_r, y_s, y_r, z_s, z_r, zd_s, zd_r,
    x_s, x_r, h_s, h_r,
):
    z, x, e = place()
    core = e % 2
    at = lambda zz, xx, ee: (zz * 4 + xx, ee)
    z1, z2, z3 = (z + 1) % 4, (z + 2) % 4, (z + 3) % 4
    plus, across, minus = (x + 1) % 4, (x + 2) % 4, (x + 3) % 4
    swap, flip = x + 1 - 2 * (x % 2), 3 - x
    x_weight = swap * (1 - core) + flip * core
    x_token = flip * (1 - core) + swap * core
    zp, zm = at(z1, x, e), at(z3, x, e)
    xp, xm = at(z, plus, e), at(z, minus, e)
    partner_w, partner_t = at(z, x_weight, e), at(z, x_token, e)
    greet(
        [zp, zm, at(z2, x, e), xp, xm, at(z, across, e)]
        + [at(z, x, (e + d) % 8) for d in range(1, 8)]
    )

    mine = pl.ds(pl.multiple_of(x * TOK, TOK), TOK)
    cols_k = lambda zz: pl.ds(pl.multiple_of(zz * 256, 256), 256)
    cols_q = lambda zz: pl.ds(pl.multiple_of(zz * 1024, 1024), 1024)
    kv_z, q_z = [], []
    for d in (1, 2, 3):
        zt = (z + d) % 4
        to = at(zt, x, e)
        kv_z.append(
            (
                remote(k_ref.at[:, cols_k(zt)], kb.at[z, mine], zs.at[0, d - 1], zr.at[0, d - 1], to),
                remote(v_ref.at[:, cols_k(zt)], vb.at[z, mine], zs.at[1, d - 1], zr.at[1, d - 1], to),
            )
        )
        q_z.append(remote(q_ref.at[:, cols_q(zt)], qb.at[z], zs.at[2, d - 1], zr.at[2, d - 1], to))
    for d in (2, 1, 3):
        for copy in kv_z[d - 1]:
            copy.start()
    own_cols = pl.ds(pl.multiple_of(e * BLK, 128), BLK)
    own_rows = pl.ds(pl.multiple_of(x * 256, 256), 256)
    local = [
        pltpu.make_async_copy(k_ref.at[:, cols_k(z)], kb.at[z, mine], lsem.at[0]),
        pltpu.make_async_copy(v_ref.at[:, cols_k(z)], vb.at[z, mine], lsem.at[1]),
        pltpu.make_async_copy(q_ref.at[:, cols_q(z)], qb.at[z], lsem.at[2]),
        pltpu.make_async_copy(op_ref.at[:, own_cols], wb.at[e, own_rows], lsem.at[3]),
    ]
    for copy in local:
        copy.start()
    w_x = [
        remote(op_ref.at[:, own_cols], wb.at[e, own_rows], o_s.at[i], o_r.at[i], at(z, xx, e))
        for i, xx in enumerate((plus, across, minus))
    ]
    for copy in w_x:
        copy.start()
    for d in (2, 1, 3):
        q_z[d - 1].start()
    local[0].wait()
    local[1].wait()

    rows = lambda xx: pl.ds(pl.multiple_of(xx * TOK, TOK), TOK)
    near, far = [], []
    for d in (0, 1, 2, 3):
        zz = (z + 4 - d) % 4
        near.append(
            [
                remote(kb.at[zz, mine], kb.at[zz, mine], xs.at[0, d], xr.at[0, d], xp),
                remote(vb.at[zz, mine], vb.at[zz, mine], xs.at[1, d], xr.at[1, d], xp),
                remote(kb.at[zz, mine], kb.at[zz, mine], xs.at[2, d], xr.at[2, d], xm),
                remote(vb.at[zz, mine], vb.at[zz, mine], xs.at[3, d], xr.at[3, d], xm),
            ]
        )
        left, right = rows(minus), rows(plus)
        far.append(
            [
                remote(kb.at[zz, left], kb.at[zz, left], xs.at[4, d], xr.at[4, d], xp),
                remote(vb.at[zz, right], vb.at[zz, right], xs.at[5, d], xr.at[5, d], xm),
            ]
        )
    order = (0, 1, 3, 2)
    for d in order:
        if d:
            kv_z[d - 1][0].wait_recv()
            kv_z[d - 1][1].wait_recv()
        for copy in near[d]:
            copy.start()
    y_up, y_down = (e + 2) % 8, (e + 6) % 8
    other = e + 1 - 2 * core
    upper, lower = pl.ds(0, 512), pl.ds(512, 512)
    w_y = [
        remote(wb.at[e], wb.at[e], o_s.at[3], o_r.at[3], at(z, x, y_up)),
        remote(wb.at[e], wb.at[e], o_s.at[4], o_r.at[4], at(z, x, y_down)),
        remote(wb.at[y_down, upper], wb.at[y_down, upper], o_s.at[5], o_r.at[5], at(z, x, y_up)),
        remote(wb.at[y_up, lower], wb.at[y_up, lower], o_s.at[6], o_r.at[6], at(z, x, y_down)),
    ]
    w_c = [
        remote(wb.at[ee], wb.at[ee], o_s.at[7 + i], o_r.at[7 + i], at(z, x, other))
        for i, ee in enumerate((e, y_down, y_up, (e + 4) % 8))
    ]
    local[3].wait()
    for copy in w_x:
        copy.wait_recv()
    w_y[0].start()
    w_y[1].start()
    w_c[0].start()
    for d in order:
        near[d][0].wait_recv()
        far[d][0].start()
        near[d][3].wait_recv()
        far[d][1].start()
    local[2].wait()
    for d in (1, 3, 2):
        q_z[d - 1].wait_recv()
    for d in order:
        near[d][1].wait_recv()
        near[d][2].wait_recv()
        far[d][0].wait_recv()
        far[d][1].wait_recv()

    own_w, far_w = [], []
    for c in range(2):
        cols = pl.ds(c * 256, 256)
        for i, (hbm, buf) in enumerate(((wg_hbm, wg), (wu_hbm, wu))):
            own_w.append(pltpu.make_async_copy(hbm.at[:, cols], buf.at[c], lsem.at[4 + 2 * c + i]))
            far_w.append(
                remote(hbm.at[:, cols], buf.at[2 + c], w_s.at[2 * c + i], w_r.at[2 * c + i], partner_w)
            )
    for copy in far_w + own_w:
        copy.start()

    bound = len_ref[0, 0]
    second = len_ref[0, 1]
    scale = HEAD_DIM ** (-0.5) * 1.4426950408889634

    def query_step(zq, _):
        q_all = qb[zq]
        stacked = [
            jnp.concatenate(
                [q_all[:, (4 * h + j) * 128 : (4 * h + j + 1) * 128] for j in range(4)], axis=0
            )
            for h in range(2)
        ]
        qpos = (zq * 4 + x) * TOK + lax.broadcasted_iota(jnp.int32, (TOK, 512), 0)
        first = jnp.where(qpos >= bound, bound, 0)

        def key_step(kz, carry):
            kpos = kz * 512 + lax.broadcasted_iota(jnp.int32, (TOK, 512), 1)
            bias = jnp.where(jnp.logical_and(kpos <= qpos, kpos >= first), 0.0, NEG)
            out = []
            for h in range(2):
                m, l, acc = carry[h]
                sc = rhs_t(stacked[h], kb[kz, :, h * 128 : (h + 1) * 128])
                sc = (sc.reshape(4, TOK, 512) + bias[None]).reshape(512, 512)
                mn = jnp.maximum(m, jnp.max(sc, axis=1, keepdims=True))
                p = jnp.exp2((sc - mn) * scale)
                a = jnp.exp2((m - mn) * scale)
                l = a * l + jnp.sum(p, axis=1, keepdims=True)
                acc = a * acc + mm(p.astype(BF16), vb[kz, :, h * 128 : (h + 1) * 128])
                out.append((mn, l, acc))
            return tuple(out)

        start = (
            jnp.full((512, 1), NEG, F32),
            jnp.zeros((512, 1), F32),
            jnp.zeros((512, 128), F32),
        )
        done = lax.fori_loop(0, zq + 1, key_step, (start, start))
        for h in range(2):
            _, l, acc = done[h]
            out = (acc / l).astype(BF16)
            for j in range(4):
                att[zq, :, (4 * h + j) * 128 : (4 * h + j + 1) * 128] = out[j * 128 : (j + 1) * 128]
        return 0

    w_y[0].wait_recv()
    w_y[2].start()
    w_y[1].wait_recv()
    w_y[3].start()
    w_c[1].start()
    w_c[2].start()
    lax.fori_loop(0, 4, query_step, 0)
    w_y[2].wait_recv()
    w_y[3].wait_recv()
    w_c[3].start()
    for copy in w_c:
        copy.wait_recv()

    ids = lax.broadcasted_iota(jnp.int32, (TOK, EXPERTS), 1)
    hot = [ids == routes[:, k : k + 1] for k in range(2)]
    named = jnp.where(jnp.logical_or(hot[0], hot[1]), 1.0, 0.0).astype(BF16)
    earlier = jnp.where(
        lax.broadcasted_iota(jnp.int32, (TOK, TOK), 1) < lax.broadcasted_iota(jnp.int32, (TOK, TOK), 0),
        1.0,
        0.0,
    ).astype(BF16)
    before = mm(earlier, named)
    slot_ids = lax.broadcasted_iota(jnp.int32, (TOK, ROWS), 1)
    slot_hot = []
    for k in range(2):
        rank = jnp.sum(jnp.where(hot[k], before, 0.0), axis=1, keepdims=True).astype(jnp.int32)
        expert = routes[:, k : k + 1]
        slot = jnp.where(
            rank < MAIN, expert * MAIN + rank, EXPERTS * MAIN + expert * 2 + (rank - MAIN)
        )
        slot_hot.append(jnp.where(slot_ids == slot, 1.0, 0.0).astype(BF16))
    slot_any = slot_hot[0] + slot_hot[1]
    tpos = (z * 4 + x) * TOK + lax.broadcasted_iota(jnp.int32, (TOK, 1), 0)
    in_second = tpos >= bound
    own_len = jnp.where(in_second, second, bound).astype(F32)
    tall = lax.broadcasted_iota(jnp.int32, (TOK, REST), 0)
    wide = lax.broadcasted_iota(jnp.int32, (TOK, REST), 1)
    base = (wide // 2) * 16 + (wide % 2) * 8
    picks = [jnp.where(tall == base + kk, 1.0, 0.0).astype(BF16) for kk in range(6)]
    tall_t = lax.broadcasted_iota(jnp.int32, (REST, TOK), 0)
    wide_t = lax.broadcasted_iota(jnp.int32, (REST, TOK), 1)
    base_t = (tall_t // 2) * 16 + (tall_t % 2) * 8
    picks_t = [jnp.where(wide_t == base_t + kk, 1.0, 0.0).astype(BF16) for kk in range(6)]

    rsc = [
        [
            remote(part.at[c, i], rs.at[c, i], rs_s.at[c, i], rs_r.at[c, i], zp if i % 2 == 0 else zm)
            for i in range(6)
        ]
        for c in range(CHUNKS)
    ]

    def project(target, block):
        return mm(att[target], wb[block])

    def s1(c):
        for half in range(2):
            part[c, half] = project(z2, 2 * c + half).astype(BF16)
            rsc[c][half].start()

    def s2(c):
        part[c, 2] = project(z1, 2 * c + 1).astype(BF16)
        rsc[c][2].start()
        part[c, 3] = project(z3, 2 * c).astype(BF16)
        rsc[c][3].start()

    def s3(c):
        for half, target in ((0, z1), (1, z3)):
            through = project(target, 2 * c + half)
            rsc[c][half].wait_recv()
            part[c, 4 + half] = (through + rs[c, half].astype(F32)).astype(BF16)
            rsc[c][4 + half].start()

    state = {"square": jnp.zeros((TOK, 1), F32), "logits": jnp.zeros((TOK, EXPERTS), F32)}

    def s4(c):
        sums = []
        for half in range(2):
            span = slice((2 * c + half) * BLK, (2 * c + half + 1) * BLK)
            sums.append(res[:, span].astype(F32) + project(z, 2 * c + half))
        for i in (2, 3, 4, 5):
            rsc[c][i].wait_recv()
        for half, terms in ((0, (3, 4)), (1, (2, 5))):
            span = slice((2 * c + half) * BLK, (2 * c + half + 1) * BLK)
            h = sums[half] + rs[c, terms[0]].astype(F32) + rs[c, terms[1]].astype(F32)
            hid[:, span] = h
            state["square"] = state["square"] + jnp.sum(h * h, axis=1, keepdims=True)
            nrm[:, span] = (h * gain[:, span]).astype(BF16)
        span = slice(c * CW, (c + 1) * CW)
        r_all = router[:, span]
        r_hi = r_all.astype(BF16)
        r_rest = r_all - r_hi.astype(F32)
        r_mid = r_rest.astype(BF16)
        r_low = (r_rest - r_mid.astype(F32)).astype(BF16)
        rows_c = nrm[:, span]
        state["logits"] = (
            state["logits"] + rhs_t(rows_c, r_hi) + rhs_t(rows_c, r_mid) + rhs_t(rows_c, r_low)
        )

    own_slot = 2 * z
    my_rows = pl.ds(pl.multiple_of(e * MAIN, MAIN), MAIN)
    last = CHUNKS - 1
    wide_cols = lambda c: pl.ds(c * CW, CW + (EXT if c == last else 0))
    pack_cols = lambda c: pl.ds(c * 128, 256 if c == last else 128)
    y_copies, keep = [], []
    for c in range(CHUNKS):
        copies = []
        for d in range(1, 8):
            et = (e + d) % 8
            to = at(z, x, et)
            copies.append(
                remote(
                    stage.at[pl.ds(pl.multiple_of(et * MAIN, MAIN), MAIN), wide_cols(c)],
                    xb.at[own_slot, my_rows, wide_cols(c)],
                    y_s.at[c, 0, d - 1],
                    y_r.at[c, 0, d - 1],
                    to,
                )
            )
            copies.append(
                remote(
                    pack.at[et, :, pack_cols(c)],
                    unpack.at[e, :, pack_cols(c)],
                    y_s.at[c, 1, d - 1],
                    y_r.at[c, 1, d - 1],
                    to,
                )
            )
        y_copies.append(copies)
        keep.append(
            [
                pltpu.make_async_copy(
                    stage.at[my_rows, wide_cols(c)],
                    xb.at[own_slot, my_rows, wide_cols(c)],
                    lsem.at[8 + 2 * c],
                ),
                pltpu.make_async_copy(
                    pack.at[e, :, pack_cols(c)], unpack.at[e, :, pack_cols(c)], lsem.at[9 + 2 * c]
                ),
            ]
        )

    def scaled_ext():
        norm_scale = lax.rsqrt(state["square"] * (1.0 / D) + 1e-05)
        logits = state["logits"] * norm_scale
        picked = [jnp.sum(jnp.where(hot[k], logits, 0.0), axis=1, keepdims=True) for k in range(2)]
        gates = [
            1.0 / (1.0 + jnp.exp(picked[1] - picked[0])),
            1.0 / (1.0 + jnp.exp(picked[0] - picked[1])),
        ]
        lanes = lax.broadcasted_iota(jnp.int32, (TOK, EXT), 1)
        s_hi = norm_scale.astype(BF16).astype(F32)
        s_low = norm_scale - s_hi
        scales = jnp.where(lanes == 16, s_hi, jnp.where(lanes == 17, s_low, 0.0)).astype(BF16)
        ext = lhs_t(slot_any, scales)
        bucket = jnp.where(in_second, 8, 0) + e
        for k in range(2):
            weight = (gates[k] / own_len).astype(BF16).astype(F32)
            ext = ext + lhs_t(slot_hot[k], jnp.where(lanes == bucket, weight, 0.0).astype(BF16))
        stage[:, D:] = ext.astype(BF16)

    def send_y(c):
        span = slice(c * CW, (c + 1) * CW)
        stage[:, span] = lhs_t(slot_any, nrm[:, span]).astype(BF16)
        if c == last:
            scaled_ext()
        got = jnp.zeros((TOK, 128), F32)
        for kk in range(6):
            col = c * CW + kk * 128
            got = got + mm(picks[kk], stage[EXPERTS * MAIN :, col : col + 128])
        pack[:, :, c * 128 : (c + 1) * 128] = got.astype(BF16).reshape(EXPERTS, 16, 128)
        if c == last:
            got = mm(picks[0], stage[EXPERTS * MAIN :, D:])
            pack[:, :, (c + 1) * 128 : (c + 2) * 128] = got.astype(BF16).reshape(EXPERTS, 16, 128)
        for copy in y_copies[c] + keep[c]:
            copy.start()

    slot_of = lambda d: 2 * ((z + 4 - d) % 4)
    top, bottom = pl.ds(0, 128), pl.ds(128, ROWS - 128)

    def ring(c, side, s_sem, r_sem):
        cw = wide_cols(c)
        o, a, b = own_slot + side, slot_of(1) + side, slot_of(3) + side
        return [
            remote(xb.at[o, :, cw], xb.at[o, :, cw], s_sem(0), r_sem(0), zp),
            remote(xb.at[o, :, cw], xb.at[o, :, cw], s_sem(1), r_sem(1), zm),
            remote(xb.at[a, top, cw], xb.at[a, top, cw], s_sem(2), r_sem(2), zp),
            remote(xb.at[b, bottom, cw], xb.at[b, bottom, cw], s_sem(3), r_sem(3), zm),
        ]

    zc = [
        ring(c, 0, lambda i, c=c: z_s.at[c, i], lambda i, c=c: z_r.at[c, i]) for c in range(CHUNKS)
    ]
    zd = {
        c: ring(c, 1, lambda i, n=n: zd_s.at[n, i], lambda i, n=n: zd_r.at[n, i])
        for n, c in enumerate(X_FIRST)
    }
    xc = [
        [
            remote(
                xb.at[slot_of(d), :, wide_cols(c)],
                xb.at[slot_of(d) + 1, :, wide_cols(c)],
                x_s.at[c, d],
                x_r.at[c, d],
                partner_t,
            )
            for d in range(1 if c in X_FIRST else 4)
        ]
        for c in range(CHUNKS)
    ]

    def take_y(c):
        for copy in keep[c]:
            copy.wait()
        for copy in y_copies[c]:
            copy.wait_recv()
        flat = unpack[:, :, c * 128 : (c + 1) * 128].reshape(TOK, 128)
        for kk in range(6):
            col = c * CW + kk * 128
            xb[own_slot, EXPERTS * MAIN :, col : col + 128] = mm(picks_t[kk], flat).astype(BF16)
        if c == last:
            flat = unpack[:, :, (c + 1) * 128 : (c + 2) * 128].reshape(TOK, 128)
            xb[own_slot, EXPERTS * MAIN :, D:] = mm(picks_t[0], flat).astype(BF16)
        xc[c][0].start()
        zc[c][0].start()
        zc[c][1].start()

    def pass_x(c):
        xc[c][0].wait_recv()
        zd[c][0].start()
        zd[c][1].start()

    def pass_z(c):
        zc[c][0].wait_recv()
        zc[c][2].start()
        zc[c][1].wait_recv()
        zc[c][3].start()
        if c not in X_FIRST:
            xc[c][1].start()
            xc[c][3].start()

    def pass_zd(c):
        zd[c][0].wait_recv()
        zd[c][2].start()
        zd[c][1].wait_recv()
        zd[c][3].start()

    def pass_far(c):
        zc[c][2].wait_recv()
        zc[c][3].wait_recv()
        if c not in X_FIRST:
            xc[c][2].start()

    def experts(slot):
        def chunk_step(c, _):
            rows_x = xb[slot, :, :D]
            ext = xb[slot, :, D:]
            row_scale = ext[:, 16:17].astype(F32) + ext[:, 17:18].astype(F32)
            gate = mm(rows_x, wg[c]) * row_scale
            up = mm(rows_x, wu[c]) * row_scale
            act = (gate / (1.0 + jnp.exp(-gate)) * up).astype(BF16)
            hs[c] = hs[c] + lhs_t(ext, act)
            return 0

        lax.fori_loop(0, 4, chunk_step, 0)

    s1(0)
    s2(0)
    s1(1)
    s2(1)
    s3(0)
    s1(2)
    s2(2)
    s3(1)
    s4(0)
    send_y(0)
    s1(3)
    s2(3)
    s3(2)
    s4(1)
    send_y(1)
    take_y(0)
    s3(3)
    s4(2)
    send_y(2)
    take_y(1)
    s4(3)
    send_y(3)
    pass_z(0)
    take_y(2)
    pass_x(1)
    inv = 1.0 / own_len
    pool_out[...] = jnp.zeros_like(pool_out)
    pool_out[0:1] = jnp.sum(hid[...] * jnp.where(in_second, 0.0, inv), axis=0, keepdims=True)
    pool_out[1:2] = jnp.sum(hid[...] * jnp.where(in_second, inv, 0.0), axis=0, keepdims=True)
    hs[...] = jnp.zeros_like(hs)
    take_y(3)
    pass_z(1)
    pass_z(2)
    pass_zd(1)
    for copy in own_w:
        copy.wait()
    pass_z(3)
    for copy in far_w:
        copy.wait_recv()
    pass_far(0)
    experts(own_slot)
    pass_far(1)
    pass_far(2)
    for c in range(CHUNKS):
        if c not in X_FIRST:
            xc[c][0].wait_recv()
    experts(own_slot + 1)
    pass_far(3)
    experts(slot_of(1))
    experts(slot_of(3))
    experts(slot_of(2))
    for d in (1, 3, 2):
        for c in range(CHUNKS):
            if c not in X_FIRST:
                xc[c][d].wait_recv()
            elif d == 2:
                zd[c][2].wait_recv()
                zd[c][3].wait_recv()
        experts(slot_of(d) + 1)

    home = remote(hs.at[pl.ds(2, 2), pl.ds(0, 16)], hr, h_s, h_r, partner_w)
    home.start()
    home.wait_recv()
    for c in range(2):
        hs_out[:, c * 256 : (c + 1) * 256] = hs[c, 0:16] + hr[c]
    home.wait_send()
    started = [*q_z, *w_x, *w_y, *w_c, *far_w]
    for group in (*kv_z, *near, *far, *rsc, *y_copies, *zc, *zd.values(), *xc):
        started.extend(group)
    for copy in started:
        copy.wait_send()


def layer(lengths, q, k, v, op, res, gain, router_t, routes, w_gate, w_up):
    vmem = pl.BlockSpec(memory_space=pltpu.VMEM)
    hbm = pl.BlockSpec(memory_space=pl.ANY)
    dma = pltpu.SemaphoreType.DMA
    return pl.pallas_call(
        layer_kernel,
        out_shape=(
            jax.ShapeDtypeStruct((16, 512), F32),
            jax.ShapeDtypeStruct((8, D), F32),
        ),
        in_specs=[pl.BlockSpec(memory_space=pltpu.SMEM)] + [hbm] * 4 + [vmem] * 4 + [hbm, hbm],
        out_specs=(vmem, vmem),
        scratch_shapes=[
            pltpu.VMEM((4, TOK, 1024), BF16),
            pltpu.VMEM((4, 512, 256), BF16),
            pltpu.VMEM((4, 512, 256), BF16),
            pltpu.VMEM((4, TOK, 1024), BF16),
            pltpu.VMEM((8, 1024, BLK), BF16),
            pltpu.VMEM((CHUNKS, 6, TOK, BLK), BF16),
            pltpu.VMEM((CHUNKS, 6, TOK, BLK), BF16),
            pltpu.VMEM((TOK, D), F32),
            pltpu.VMEM((TOK, D), BF16),
            pltpu.VMEM((ROWS, WIDE), BF16),
            pltpu.VMEM((EXPERTS, 16, 128 * (CHUNKS + 1)), BF16),
            pltpu.VMEM((EXPERTS, 16, 128 * (CHUNKS + 1)), BF16),
            pltpu.VMEM((8, ROWS, WIDE), BF16),
            pltpu.VMEM((4, D, 256), BF16),
            pltpu.VMEM((4, D, 256), BF16),
            pltpu.VMEM((4, EXT, 256), F32),
            pltpu.VMEM((2, 16, 256), F32),
            dma((8 + 2 * CHUNKS,)),
            dma((3, 3)), dma((3, 3)),
            dma((6, 4)), dma((6, 4)),
            dma((11,)), dma((11,)),
            dma((CHUNKS, 6)), dma((CHUNKS, 6)),
            dma((4,)), dma((4,)),
            dma((CHUNKS, 2, 7)), dma((CHUNKS, 2, 7)),
            dma((CHUNKS, 4)), dma((CHUNKS, 4)),
            dma((max(1, len(X_FIRST)), 4)), dma((max(1, len(X_FIRST)), 4)),
            dma((CHUNKS, 4)), dma((CHUNKS, 4)),
            dma, dma,
        ],
        compiler_params=pltpu.CompilerParams(
            collective_id=0, has_side_effects=True, vmem_limit_bytes=VMEM_LIMIT
        ),
        cost_estimate=pl.CostEstimate(
            flops=36_000_000_000, bytes_accessed=24_000_000, transcendentals=8_000_000
        ),
        name="layer",
    )(lengths, q, k, v, op, res, gain, router_t, routes, w_gate, w_up)


def final_kernel(
    hs, pool, vec, head, wd, chosen, rejected,
    rew_out, loss_out, gh_out, wt_out,
    r_mine, r_exp, r_sum, r_seq, g_mine, g_exp, g_sum, g_seq,
    re_s, re_r, rq_s, rq_r, ge_s, ge_r, gq_s, gq_r,
):
    s = lax.axis_index("seq")
    e = lax.axis_index("exp")
    exp_peers = [(s, (e + d) % 8) for d in range(1, 8)]
    seq_peers = [((s + d) % 16, e) for d in range(1, 16)]
    greet(exp_peers + seq_peers)

    def all_sum(mine, got_exp, total, got_seq, es, er, qs, qr):
        copies = [
            remote(mine, got_exp.at[i], es.at[i], er.at[i], to) for i, to in enumerate(exp_peers)
        ]
        for copy in copies:
            copy.start()
        acc = mine[...]
        for i, copy in enumerate(copies):
            copy.wait_recv()
            acc = acc + got_exp[i]
        total[...] = acc
        more = [
            remote(total, got_seq.at[i], qs.at[i], qr.at[i], to) for i, to in enumerate(seq_peers)
        ]
        for copy in more:
            copy.start()
        for i, copy in enumerate(more):
            copy.wait_recv()
            acc = acc + got_seq[i]
        return acc, copies + more

    hsv = hs[...]
    part = jnp.sum(hsv * vec[...], axis=1, keepdims=True)
    own = jnp.sum(pool[...] * head[...], axis=1, keepdims=True)
    group = lax.broadcasted_iota(jnp.int32, (8, 128), 0)
    r_mine[0:8] = part[0:8] + jnp.where(group == e, own[0:1], 0.0)
    r_mine[8:16] = part[8:16] + jnp.where(group == e, own[1:2], 0.0)
    rewards, sent = all_sum(r_mine, r_exp, r_sum, r_seq, re_s, re_r, rq_s, rq_r)
    rew_out[...] = rewards

    r0, r1 = rewards[0:8], rewards[8:16]
    ch, rj = chosen[...], rejected[...]
    margin = jnp.where(ch == 0, r0, r1) - jnp.where(rj == 0, r0, r1)
    real = lax.broadcasted_iota(jnp.int32, (8, 128), 1) < 4
    loss = jnp.maximum(-margin, 0.0) + jnp.log1p(jnp.exp(-jnp.abs(margin)))
    loss = jnp.sum(jnp.where(real, loss, 0.0), axis=1, keepdims=True)
    loss = jnp.sum(loss, axis=0, keepdims=True) * (1.0 / 32.0)
    loss_out[...] = jnp.broadcast_to(loss, (8, 128))
    factor = jnp.where(real, -1.0 / (1.0 + jnp.exp(margin)) * (1.0 / 32.0), 0.0)
    up0 = jnp.where(ch == 0, factor, 0.0) - jnp.where(rj == 0, factor, 0.0)
    up1 = jnp.where(ch == 1, factor, 0.0) - jnp.where(rj == 1, factor, 0.0)
    rg0 = jnp.sum(up0, axis=1, keepdims=True)
    rg1 = jnp.sum(up1, axis=1, keepdims=True)
    weighted = jnp.sum(hsv[0:8] * rg0 + hsv[8:16] * rg1, axis=0, keepdims=True)
    wt_out[...] = jnp.broadcast_to(weighted, (8, 512))
    hi = weighted.astype(BF16).astype(F32)
    mid = (weighted - hi).astype(BF16).astype(F32)
    low = weighted - hi - mid
    line = lax.broadcasted_iota(jnp.int32, (16, 512), 0)
    three = jnp.where(line == 0, hi, jnp.where(line == 1, mid, jnp.where(line == 2, low, 0.0)))
    moved = jnp.sum(mm(three.astype(BF16), wd[...]), axis=0, keepdims=True)
    mine = lax.broadcasted_iota(jnp.int32, (8, 1), 0) == e
    own0 = jnp.sum(jnp.where(mine, rg0, 0.0), axis=0, keepdims=True)
    own1 = jnp.sum(jnp.where(mine, rg1, 0.0), axis=0, keepdims=True)
    grad = moved + own0 * pool[0:1] + own1 * pool[1:2]
    for i in range(24):
        g_mine[i : i + 1] = grad[:, i * 128 : (i + 1) * 128]
    total, more = all_sum(g_mine, g_exp, g_sum, g_seq, ge_s, ge_r, gq_s, gq_r)
    gh_out[...] = total
    for copy in sent + more:
        copy.wait_send()


def final(hs, pool, vec, head, wd, chosen, rejected):
    vmem = pl.BlockSpec(memory_space=pltpu.VMEM)
    dma = pltpu.SemaphoreType.DMA
    return pl.pallas_call(
        final_kernel,
        out_shape=(
            jax.ShapeDtypeStruct((16, 128), F32),
            jax.ShapeDtypeStruct((8, 128), F32),
            jax.ShapeDtypeStruct((24, 128), F32),
            jax.ShapeDtypeStruct((8, 512), F32),
        ),
        in_specs=[vmem] * 7,
        out_specs=(vmem,) * 4,
        scratch_shapes=[
            pltpu.VMEM((16, 128), F32), pltpu.VMEM((7, 16, 128), F32),
            pltpu.VMEM((16, 128), F32), pltpu.VMEM((15, 16, 128), F32),
            pltpu.VMEM((24, 128), F32), pltpu.VMEM((7, 24, 128), F32),
            pltpu.VMEM((24, 128), F32), pltpu.VMEM((15, 24, 128), F32),
            dma((7,)), dma((7,)), dma((15,)), dma((15,)),
            dma((7,)), dma((7,)), dma((15,)), dma((15,)),
        ],
        compiler_params=pltpu.CompilerParams(
            collective_id=1, has_side_effects=True, vmem_limit_bytes=VMEM_LIMIT
        ),
        name="final",
    )(hs, pool, vec, head, wd, chosen, rejected)


def per_device(
    query_states, key_states, value_states, residual, out_proj, norm_gain, router,
    w_gate, w_up, w_down, reward_head, lengths, routes, pair_list,
):
    vec = jnp.sum(w_down[0].astype(F32) * reward_head[None, :], axis=1)[None, :]
    hs, pool = layer(
        lengths, query_states[0], key_states[0], value_states[0], out_proj, residual[0],
        norm_gain[None, :], router.T, routes[0], w_gate[0], w_up[0],
    )
    pad = ((0, 0), (0, 124))
    rew, loss, gh, wt = final(
        hs, pool, vec, reward_head[None, :], w_down[0],
        jnp.pad(pair_list[:, :, 0], pad), jnp.pad(pair_list[:, :, 1], pad),
    )
    rewards = rew[:, 0].reshape(2, 8).T
    grad_down = (wt[0][:, None] * reward_head[None, :]).astype(BF16)[None]
    return rewards, loss[0, 0], gh.reshape(-1), grad_down


def solution(mesh):
    placed = (
        P("exp", "seq", None), P("exp", "seq", None), P("exp", "seq", None), P("exp", "seq", None),
        P("seq", None), P(), P(), P("exp", None, "seq"), P("exp", None, "seq"),
        P("exp", "seq", None), P(), P("exp", None), P("exp", "seq", None), P(),
    )
    return jax.shard_map(
        per_device,
        mesh=mesh,
        in_specs=placed,
        out_specs=(P(), P(), P(), P("exp", "seq", None)),
        check_vma=False,
    )
```

time: 296 us -> 227 us (0.77)
  Pallas kernels: 252 us -> 214 us
  waiting for transfers between devices: 15.3 us -> 0 us
  between operations: 14.1 us -> 0.69 us
    pallas_call x2 -> x1, Pallas kernels: 226 us -> 185 us  [layer(): pl.pallas_call(layer_kernel, out_shape=(jax.ShapeDtypeStruct((16, 512), F...]
    all_gather x1 -> x0, waiting for transfers between devices: 14.7 us -> none  [per_device(): lax.all_gather(out_proj, 'seq', axis=0, tiled=True, axis_index_groups=col...]
    pallas_call x1, Pallas kernels: 26 us -> 29 us  [final(): pl.pallas_call(final_kernel, out_shape=(jax.ShapeDtypeStruct((16, 128), F...]
  transfers between devices with their start and end apart: 1 -> 0, of which waited for: 1 -> 0; matrix products, arithmetic and copies ran while one was open for 2% -> 0% of each run, Pallas kernels for 21% -> 0%
where the time goes in v2:
time: 227 us; the launch traced here: 226 us
  Pallas kernels  214 us (94%)
  local copies, waits for them, and re-layouts  6.09 us (3%)
  other arithmetic  5.52 us (2%)
    pallas_call x1, Pallas kernels, layer(): pl.pallas_call(layer_kernel, out_shape=(jax.ShapeDtypeStruct((16, 512), F...  185 us
    pallas_call x1, Pallas kernels, final(): pl.pallas_call(final_kernel, out_shape=(jax.ShapeDtypeStruct((16, 128), F...  29 us

profile of v2, /device:TPU:0, one launch (start us, length us, event | category | flops | bytes accessed | tf_op | source)
XLA Modules:
  0.0 226.4 jit_solution(7488049292300130285)
XLA Ops:
  0.6 0.0 copy-start.2
  0.6 0.0 copy-start.3
  0.7 3.2 %multiply_reduce_fusion = f32[512]{0:T(512)} fusion(f32[3072]{0:T(1024)} %param.24, bf16[1,512,3072]{2,1,0:T(8,128)(2,1)} %param.23), kind=kLoop, calls=%fused_computation.1 | loop fusion | flops 4718080 | bytes 3160064 | tf_op jit(solution)/shard_map/reduce_sum | solution.py:738
  3.8 0.0 copy-done.2
  3.8 0.1 copy.22
  3.9 0.6 pad.7.chosen
  4.5 0.1 copy.23
  4.6 0.6 pad.8.rejected
  5.2 0.0 copy-done.3
  5.2 0.7 copy.21
  5.9 185.1 %layer.1 = (f32[16,512]{1,0:T(8,128)}, f32[8,3072]{1,0:T(8,128)}) custom-call(s32[1,2]{1,0:T(1,128)} %len_ref.1, bf16[128,4096]{1,0:T(8,128)(2,1)} %bitcast.29, bf16[128,1024]{1,0:T(8,128)(2,1)} %bitcast.31, bf16[128,1024]{1,0:T(8,128)(2,1)} %bitcast.32, bf16[256,3072]{1,0:T(8,128)(2,1)} %op_ref.1, bf16[128,3072]{1,0:T(8,128)(2,1)} %bitcast.30, ...), custom_call_target="tpu_custom_call" | custom-call | flops 35999997952 | bytes 24000000 | tf_op jit(solution)/shard_map/layer/pallas_call | solution.py:583
  191.0 0.0 copy-start
  191.0 29.0 %final.1 = (f32[16,128]{1,0:T(8,128)}, f32[8,128]{1,0:T(8,128)}, f32[24,128]{1,0:T(8,128)}, f32[8,512]{1,0:T(8,128)}) custom-call(f32[16,512]{1,0:T(8,128)} %get-tuple-element.10.hs, f32[8,3072]{1,0:T(8,128)} %get-tuple-element.11.pool, f32[1,512]{1,0:T(1,128)} %bitcast.26, f32[1,3072]{1,0:T(1,128)} %bitcast.20, bf16[512,3072]{1,0:T(8,128)(2,1)} %bitcast.19, ...), custom_call_target="tpu_custom_call" | custom-call | tf_op jit(solution)/shard_map/final/pallas_call | solution.py:709
  220.1 0.0 copy-start.1
  220.1 1.2 slice.20
  221.3 0.8 slice_reduce_fusion
  222.1 0.6 reshape_squeeze.3
  222.7 0.7 slice.21
  223.5 0.0 copy-done
  223.5 2.3 %multiply_convert_fusion = bf16[1,512,3072]{2,1,0:T(8,128)(2,1)} fusion(f32[3072]{0:T(1024)S(1)} %copy-done, f32[512]{0:T(512)S(1)} %bitcast.25), kind=kLoop, calls=%fused_computation | loop fusion | flops 3145728 | bytes 3160064 | tf_op jit(solution)/shard_map/convert_element_type | solution.py:749
  225.8 0.0 copy-done.1
  225.8 0.6 copy.25
  (1 shorter events, 0.0 us)
Async XLA Ops:
  0.6 3.2 %copy-start.2 = (s32[8,4,2]{0,2,1:T(2,128)S(1)}, s32[8,4,2]{0,2,1:T(2,128)}, u32[]{:S(2)}) copy-start(s32[8,4,2]{0,2,1:T(2,128)} %param.27) | copy-start | bytes 772
  0.6 4.6 %copy-start.3 = (s32[1,128,2]{1,2,0:T(2,128)S(1)}, s32[1,128,2]{1,2,0:T(2,128)}, u32[]{:S(2)}) copy-start(s32[1,128,2]{1,2,0:T(2,128)} %param.26) | copy-start | bytes 3076
  191.0 32.4 %copy-start = (f32[3072]{0:T(1024)S(1)}, f32[3072]{0:T(1024)}, u32[]{:S(2)}) copy-start(f32[3072]{0:T(1024)} %param.24) | copy-start | bytes 36868
  220.1 5.7 %copy-start.1 = (f32[24,128]{1,0:T(8,128)S(1)}, f32[24,128]{1,0:T(8,128)}, u32[]{:S(2)}) copy-start(f32[24,128]{1,0:T(8,128)} %get-tuple-element.14) | copy-start | bytes 36868

commit v3 on v2

--- a/solution.py
+++ b/solution.py
@@ -62,12 +62,23 @@
     return jnp.dot(a, b, preferred_element_type=F32)
 
 
+def three_rows(row, width):
+    hi = row.astype(BF16).astype(F32)
+    mid = (row - hi).astype(BF16).astype(F32)
+    low = row - hi - mid
+    line = lax.broadcasted_iota(jnp.int32, (16, width), 0)
+    return jnp.where(line == 0, hi, jnp.where(line == 1, mid, jnp.where(line == 2, low, 0.0))).astype(BF16)
+
+
 def layer_kernel(
     len_ref, q_ref, k_ref, v_ref, op_ref, res, gain, router, routes, wg_hbm, wu_hbm,
-    hs_out, pool_out,
+    wd_hbm, head, pairs,
+    rew_out, loss_out, gh_out, wt_out,
     qb, kb, vb, att, wb, part, rs, hid, nrm, stage, pack, unpack, xb, wg, wu, hs, hr,
     lsem, zs, zr, xs, xr, o_s, o_r, rs_s, rs_r, w_s, w_r, y_s, y_r, z_s, z_r, zd_s, zd_r,
-    x_s, x_r, h_s, h_r,
+    x_s, x_r, h_s, h_r, wd, vec, vec_far, v_s, v_r, pool,
+    r_mine, r_exp, r_sum, r_seq, g_mine, g_exp, g_sum, g_seq,
+    re_s, re_r, rq_s, rq_r, ge_s, ge_r, gq_s, gq_r,
 ):
     z, x, e = place()
     core = e % 2
@@ -81,10 +92,11 @@
     xp, xm = at(z, plus, e), at(z, minus, e)
     partner_w, partner_t = at(z, x_weight, e), at(z, x_token, e)
     greet(
-        [zp, zm, at(z2, x, e), xp, xm, at(z, across, e)]
+        [((z * 4 + x + d) % 16, e) for d in range(1, 16)]
         + [at(z, x, (e + d) % 8) for d in range(1, 8)]
     )
 
+    wd_copy = pltpu.make_async_copy(wd_hbm, wd, lsem.at[8 + 2 * CHUNKS])
     mine = pl.ds(pl.multiple_of(x * TOK, TOK), TOK)
     cols_k = lambda zz: pl.ds(pl.multiple_of(zz * 256, 256), 256)
     cols_q = lambda zz: pl.ds(pl.multiple_of(zz * 1024, 1024), 1024)
@@ -99,24 +111,35 @@
             )
         )
         q_z.append(remote(q_ref.at[:, cols_q(zt)], qb.at[z], zs.at[2, d - 1], zr.at[2, d - 1], to))
-    for d in (2, 1, 3):
-        for copy in kv_z[d - 1]:
-            copy.start()
-    own_cols = pl.ds(pl.multiple_of(e * BLK, 128), BLK)
-    own_rows = pl.ds(pl.multiple_of(x * 256, 256), 256)
+    eighth = lambda ee: pl.ds(pl.multiple_of(ee * BLK, 128), BLK)
+    row_of = lambda xx: pl.ds(pl.multiple_of(xx * 256, 256), 256)
+    row_up = lambda xx: pl.ds(pl.multiple_of(xx * 256, 128), 128)
+    row_low = lambda xx: pl.ds(pl.multiple_of(xx * 256 + 128, 128), 128)
     local = [
         pltpu.make_async_copy(k_ref.at[:, cols_k(z)], kb.at[z, mine], lsem.at[0]),
         pltpu.make_async_copy(v_ref.at[:, cols_k(z)], vb.at[z, mine], lsem.at[1]),
         pltpu.make_async_copy(q_ref.at[:, cols_q(z)], qb.at[z], lsem.at[2]),
-        pltpu.make_async_copy(op_ref.at[:, own_cols], wb.at[e, own_rows], lsem.at[3]),
+        pltpu.make_async_copy(op_ref.at[:, eighth(e)], wb.at[row_of(x), eighth(e)], lsem.at[3]),
     ]
-    for copy in local:
-        copy.start()
-    w_x = [
-        remote(op_ref.at[:, own_cols], wb.at[e, own_rows], o_s.at[i], o_r.at[i], at(z, xx, e))
-        for i, xx in enumerate((plus, across, minus))
-    ]
-    for copy in w_x:
+    def w_ring(cols, n):
+        return [
+            remote(op_ref.at[:, cols], wb.at[row_of(x), cols], o_s.at[n], o_r.at[n], xp),
+            remote(op_ref.at[:, cols], wb.at[row_of(x), cols], o_s.at[n + 1], o_r.at[n + 1], xm),
+            remote(
+                wb.at[row_up(minus), cols], wb.at[row_up(minus), cols], o_s.at[n + 2], o_r.at[n + 2], xp
+            ),
+            remote(
+                wb.at[row_low(plus), cols], wb.at[row_low(plus), cols], o_s.at[n + 3], o_r.at[n + 3], xm
+            ),
+        ]
+
+    w_x = w_ring(eighth(e), 0)
+    w_x[0].start()
+    w_x[1].start()
+    for d in (2, 1, 3):
+        for copy in kv_z[d - 1]:
+            copy.start()
+    for copy in local + [wd_copy]:
         copy.start()
     for d in (2, 1, 3):
         q_z[d - 1].start()
@@ -142,45 +165,69 @@
                 remote(vb.at[zz, right], vb.at[zz, right], xs.at[5, d], xr.at[5, d], xm),
             ]
         )
-    order = (0, 1, 3, 2)
-    for d in order:
-        if d:
-            kv_z[d - 1][0].wait_recv()
-            kv_z[d - 1][1].wait_recv()
-        for copy in near[d]:
-            copy.start()
     y_up, y_down = (e + 2) % 8, (e + 6) % 8
     other = e + 1 - 2 * core
     upper, lower = pl.ds(0, 512), pl.ds(512, 512)
+    def over_y(part_rows, ee, n, to):
+        ref = wb.at[part_rows, eighth(ee)]
+        return remote(ref, ref, o_s.at[n], o_r.at[n], at(z, x, to))
+
     w_y = [
-        remote(wb.at[e], wb.at[e], o_s.at[3], o_r.at[3], at(z, x, y_up)),
-        remote(wb.at[e], wb.at[e], o_s.at[4], o_r.at[4], at(z, x, y_down)),
-        remote(wb.at[y_down, upper], wb.at[y_down, upper], o_s.at[5], o_r.at[5], at(z, x, y_up)),
-        remote(wb.at[y_up, lower], wb.at[y_up, lower], o_s.at[6], o_r.at[6], at(z, x, y_down)),
+        over_y(upper, e, 8, y_up),
+        over_y(lower, e, 9, y_down),
+        over_y(lower, e, 10, y_up),
+        over_y(upper, e, 11, y_down),
+        over_y(upper, y_down, 12, y_up),
+        over_y(lower, y_up, 13, y_down),
     ]
     w_c = [
-        remote(wb.at[ee], wb.at[ee], o_s.at[7 + i], o_r.at[7 + i], at(z, x, other))
-        for i, ee in enumerate((e, y_down, y_up, (e + 4) % 8))
+        remote(wb.at[:, cols], wb.at[:, cols], o_s.at[14 + i], o_r.at[14 + i], at(z, x, other))
+        for i, cols in enumerate(
+            (eighth(e), eighth(y_down), eighth(y_up), eighth((e + 4) % 8))
+        )
     ]
+    w_x[0].wait_recv()
+    w_x[2].start()
+    w_x[1].wait_recv()
+    w_x[3].start()
+    for copy in near[0]:
+        copy.start()
     local[3].wait()
-    for copy in w_x:
-        copy.wait_recv()
-    w_y[0].start()
-    w_y[1].start()
+    w_x[2].wait_recv()
+    w_x[3].wait_recv()
+    for copy in w_y[:4]:
+        copy.start()
     w_c[0].start()
+    order = (0, 1, 3, 2)
+    for d in (1, 3, 2):
+        kv_z[d - 1][0].wait_recv()
+        kv_z[d - 1][1].wait_recv()
+        for copy in near[d]:
+            copy.start()
+    wd_copy.wait()
+    vec[...] = jnp.broadcast_to(
+        jnp.sum(rhs_t(three_rows(head[...], D), wd[...]), axis=0, keepdims=True), (8, 512)
+    )
+    vec_copy = remote(vec, vec_far, v_s, v_r, partner_w)
+    vec_copy.start()
     for d in order:
         near[d][0].wait_recv()
         far[d][0].start()
         near[d][3].wait_recv()
         far[d][1].start()
-    local[2].wait()
-    for d in (1, 3, 2):
-        q_z[d - 1].wait_recv()
+        if d == 1:
+            w_y[0].wait_recv()
+            w_y[4].start()
+            w_y[1].wait_recv()
+            w_y[5].start()
     for d in order:
         near[d][1].wait_recv()
         near[d][2].wait_recv()
         far[d][0].wait_recv()
         far[d][1].wait_recv()
+    local[2].wait()
+    for d in (1, 3, 2):
+        q_z[d - 1].wait_recv()
 
     own_w, far_w = [], []
     for c in range(2):
@@ -237,19 +284,11 @@
                 att[zq, :, (4 * h + j) * 128 : (4 * h + j + 1) * 128] = out[j * 128 : (j + 1) * 128]
         return 0
 
-    w_y[0].wait_recv()
-    w_y[2].start()
-    w_y[1].wait_recv()
-    w_y[3].start()
+    query_step(z2, 0)
+    w_y[2].wait_recv()
+    w_y[3].wait_recv()
     w_c[1].start()
     w_c[2].start()
-    lax.fori_loop(0, 4, query_step, 0)
-    w_y[2].wait_recv()
-    w_y[3].wait_recv()
-    w_c[3].start()
-    for copy in w_c:
-        copy.wait_recv()
-
     ids = lax.broadcasted_iota(jnp.int32, (TOK, EXPERTS), 1)
     hot = [ids == routes[:, k : k + 1] for k in range(2)]
     named = jnp.where(jnp.logical_or(hot[0], hot[1]), 1.0, 0.0).astype(BF16)
@@ -290,7 +329,7 @@
     ]
 
     def project(target, block):
-        return mm(att[target], wb[block])
+        return mm(att[target], wb[:, block * BLK : (block + 1) * BLK])
 
     def s1(c):
         for half in range(2):
@@ -490,7 +529,7 @@
         if c not in X_FIRST:
             xc[c][2].start()
 
-    def experts(slot):
+    def experts(slot, low, high):
         def chunk_step(c, _):
             rows_x = xb[slot, :, :D]
             ext = xb[slot, :, D:]
@@ -501,21 +540,26 @@
             hs[c] = hs[c] + lhs_t(ext, act)
             return 0
 
-        lax.fori_loop(0, 4, chunk_step, 0)
-
-    s1(0)
+        lax.fori_loop(low, high, chunk_step, 0)
+
+    w_y[4].wait_recv()
+    w_y[5].wait_recv()
+    w_c[3].start()
+    for copy in w_c:
+        copy.wait_recv()
+    for c in range(CHUNKS):
+        s1(c)
+    lax.fori_loop(0, 2, lambda i, _: query_step((z1 + 2 * i) % 4, _), 0)
     s2(0)
-    s1(1)
+    s3(0)
     s2(1)
-    s3(0)
-    s1(2)
+    s3(1)
+    query_step(z, 0)
     s2(2)
-    s3(1)
+    s3(2)
     s4(0)
     send_y(0)
-    s1(3)
     s2(3)
-    s3(2)
     s4(1)
     send_y(1)
     take_y(0)
@@ -529,116 +573,49 @@
     take_y(2)
     pass_x(1)
     inv = 1.0 / own_len
-    pool_out[...] = jnp.zeros_like(pool_out)
-    pool_out[0:1] = jnp.sum(hid[...] * jnp.where(in_second, 0.0, inv), axis=0, keepdims=True)
-    pool_out[1:2] = jnp.sum(hid[...] * jnp.where(in_second, inv, 0.0), axis=0, keepdims=True)
+    pool[...] = jnp.zeros_like(pool)
+    pool[0:1] = jnp.sum(hid[...] * jnp.where(in_second, 0.0, inv), axis=0, keepdims=True)
+    pool[1:2] = jnp.sum(hid[...] * jnp.where(in_second, inv, 0.0), axis=0, keepdims=True)
     hs[...] = jnp.zeros_like(hs)
     take_y(3)
     pass_z(1)
+    for copy in own_w:
+        copy.wait()
+    experts(own_slot, 0, 2)
     pass_z(2)
     pass_zd(1)
-    for copy in own_w:
-        copy.wait()
+    for c in range(CHUNKS):
+        if c not in X_FIRST:
+            xc[c][0].wait_recv()
+    experts(own_slot + 1, 0, 2)
     pass_z(3)
     for copy in far_w:
         copy.wait_recv()
     pass_far(0)
-    experts(own_slot)
+    experts(own_slot, 2, 4)
+    experts(own_slot + 1, 2, 4)
     pass_far(1)
+    experts(slot_of(1), 0, 4)
     pass_far(2)
-    for c in range(CHUNKS):
-        if c not in X_FIRST:
-            xc[c][0].wait_recv()
-    experts(own_slot + 1)
     pass_far(3)
-    experts(slot_of(1))
-    experts(slot_of(3))
-    experts(slot_of(2))
+    experts(slot_of(3), 0, 4)
     for d in (1, 3, 2):
+        if d == 2:
+            experts(slot_of(2), 0, 4)
         for c in range(CHUNKS):
             if c not in X_FIRST:
                 xc[c][d].wait_recv()
             elif d == 2:
                 zd[c][2].wait_recv()
                 zd[c][3].wait_recv()
-        experts(slot_of(d) + 1)
+        experts(slot_of(d) + 1, 0, 4)
 
     home = remote(hs.at[pl.ds(2, 2), pl.ds(0, 16)], hr, h_s, h_r, partner_w)
     home.start()
-    home.wait_recv()
-    for c in range(2):
-        hs_out[:, c * 256 : (c + 1) * 256] = hs[c, 0:16] + hr[c]
-    home.wait_send()
-    started = [*q_z, *w_x, *w_y, *w_c, *far_w]
-    for group in (*kv_z, *near, *far, *rsc, *y_copies, *zc, *zd.values(), *xc):
-        started.extend(group)
-    for copy in started:
-        copy.wait_send()
-
-
-def layer(lengths, q, k, v, op, res, gain, router_t, routes, w_gate, w_up):
-    vmem = pl.BlockSpec(memory_space=pltpu.VMEM)
-    hbm = pl.BlockSpec(memory_space=pl.ANY)
-    dma = pltpu.SemaphoreType.DMA
-    return pl.pallas_call(
-        layer_kernel,
-        out_shape=(
-            jax.ShapeDtypeStruct((16, 512), F32),
-            jax.ShapeDtypeStruct((8, D), F32),
-        ),
-        in_specs=[pl.BlockSpec(memory_space=pltpu.SMEM)] + [hbm] * 4 + [vmem] * 4 + [hbm, hbm],
-        out_specs=(vmem, vmem),
-        scratch_shapes=[
-            pltpu.VMEM((4, TOK, 1024), BF16),
-            pltpu.VMEM((4, 512, 256), BF16),
-            pltpu.VMEM((4, 512, 256), BF16),
-            pltpu.VMEM((4, TOK, 1024), BF16),
-            pltpu.VMEM((8, 1024, BLK), BF16),
-            pltpu.VMEM((CHUNKS, 6, TOK, BLK), BF16),
-            pltpu.VMEM((CHUNKS, 6, TOK, BLK), BF16),
-            pltpu.VMEM((TOK, D), F32),
-            pltpu.VMEM((TOK, D), BF16),
-            pltpu.VMEM((ROWS, WIDE), BF16),
-            pltpu.VMEM((EXPERTS, 16, 128 * (CHUNKS + 1)), BF16),
-            pltpu.VMEM((EXPERTS, 16, 128 * (CHUNKS + 1)), BF16),
-            pltpu.VMEM((8, ROWS, WIDE), BF16),
-            pltpu.VMEM((4, D, 256), BF16),
-            pltpu.VMEM((4, D, 256), BF16),
-            pltpu.VMEM((4, EXT, 256), F32),
-            pltpu.VMEM((2, 16, 256), F32),
-            dma((8 + 2 * CHUNKS,)),
-            dma((3, 3)), dma((3, 3)),
-            dma((6, 4)), dma((6, 4)),
-            dma((11,)), dma((11,)),
-            dma((CHUNKS, 6)), dma((CHUNKS, 6)),
-            dma((4,)), dma((4,)),
-            dma((CHUNKS, 2, 7)), dma((CHUNKS, 2, 7)),
-            dma((CHUNKS, 4)), dma((CHUNKS, 4)),
-            dma((max(1, len(X_FIRST)), 4)), dma((max(1, len(X_FIRST)), 4)),
-            dma((CHUNKS, 4)), dma((CHUNKS, 4)),
-            dma, dma,
-        ],
-        compiler_params=pltpu.CompilerParams(
-            collective_id=0, has_side_effects=True, vmem_limit_bytes=VMEM_LIMIT
-        ),
-        cost_estimate=pl.CostEstimate(
-            flops=36_000_000_000, bytes_accessed=24_000_000, transcendentals=8_000_000
-        ),
-        name="layer",
-    )(lengths, q, k, v, op, res, gain, router_t, routes, w_gate, w_up)
-
-
-def final_kernel(
-    hs, pool, vec, head, wd, chosen, rejected,
-    rew_out, loss_out, gh_out, wt_out,
-    r_mine, r_exp, r_sum, r_seq, g_mine, g_exp, g_sum, g_seq,
-    re_s, re_r, rq_s, rq_r, ge_s, ge_r, gq_s, gq_r,
-):
-    s = lax.axis_index("seq")
-    e = lax.axis_index("exp")
+    vec_copy.wait_recv()
+    s = z * 4 + x
     exp_peers = [(s, (e + d) % 8) for d in range(1, 8)]
     seq_peers = [((s + d) % 16, e) for d in range(1, 16)]
-    greet(exp_peers + seq_peers)
 
     def all_sum(mine, got_exp, total, got_seq, es, er, qs, qr):
         copies = [
@@ -661,62 +638,96 @@
             acc = acc + got_seq[i]
         return acc, copies + more
 
-    hsv = hs[...]
-    part = jnp.sum(hsv * vec[...], axis=1, keepdims=True)
+    part_r = jnp.zeros((16, 1), F32)
+    for c in range(2):
+        span = slice(c * 256, (c + 1) * 256)
+        part_r = part_r + jnp.sum(
+            hs[c, 0:16] * vec[0:1, span] + hs[2 + c, 0:16] * vec_far[0:1, span], axis=1, keepdims=True
+        )
     own = jnp.sum(pool[...] * head[...], axis=1, keepdims=True)
     group = lax.broadcasted_iota(jnp.int32, (8, 128), 0)
-    r_mine[0:8] = part[0:8] + jnp.where(group == e, own[0:1], 0.0)
-    r_mine[8:16] = part[8:16] + jnp.where(group == e, own[1:2], 0.0)
+    r_mine[0:8] = part_r[0:8] + jnp.where(group == e, own[0:1], 0.0)
+    r_mine[8:16] = part_r[8:16] + jnp.where(group == e, own[1:2], 0.0)
     rewards, sent = all_sum(r_mine, r_exp, r_sum, r_seq, re_s, re_r, rq_s, rq_r)
-    rew_out[...] = rewards
-
+
+    home.wait_recv()
+    hsv = jnp.concatenate([hs[c, 0:16] + hr[c] for c in range(2)], axis=1)
     r0, r1 = rewards[0:8], rewards[8:16]
-    ch, rj = chosen[...], rejected[...]
-    margin = jnp.where(ch == 0, r0, r1) - jnp.where(rj == 0, r0, r1)
-    real = lax.broadcasted_iota(jnp.int32, (8, 128), 1) < 4
+    lane = lax.broadcasted_iota(jnp.int32, (8, 128), 1)
+    rew_out[...] = jnp.where(lane == 0, r0, r1)[:, :2]
+    named_pair = pairs[...]
+    value = jnp.where(named_pair == 0, r0, r1)
+    margin = value - pltpu.roll(value, 127, 1)
+    real = jnp.logical_and(lane % 2 == 0, lane < 8)
     loss = jnp.maximum(-margin, 0.0) + jnp.log1p(jnp.exp(-jnp.abs(margin)))
     loss = jnp.sum(jnp.where(real, loss, 0.0), axis=1, keepdims=True)
-    loss = jnp.sum(loss, axis=0, keepdims=True) * (1.0 / 32.0)
-    loss_out[...] = jnp.broadcast_to(loss, (8, 128))
+    loss_out[...] = jnp.sum(loss, axis=0, keepdims=True) * (1.0 / 32.0)
     factor = jnp.where(real, -1.0 / (1.0 + jnp.exp(margin)) * (1.0 / 32.0), 0.0)
-    up0 = jnp.where(ch == 0, factor, 0.0) - jnp.where(rj == 0, factor, 0.0)
-    up1 = jnp.where(ch == 1, factor, 0.0) - jnp.where(rj == 1, factor, 0.0)
-    rg0 = jnp.sum(up0, axis=1, keepdims=True)
-    rg1 = jnp.sum(up1, axis=1, keepdims=True)
+    factor = factor - pltpu.roll(factor, 1, 1)
+    rg0 = jnp.sum(jnp.where(named_pair == 0, factor, 0.0), axis=1, keepdims=True)
+    rg1 = jnp.sum(jnp.where(named_pair == 1, factor, 0.0), axis=1, keepdims=True)
     weighted = jnp.sum(hsv[0:8] * rg0 + hsv[8:16] * rg1, axis=0, keepdims=True)
-    wt_out[...] = jnp.broadcast_to(weighted, (8, 512))
-    hi = weighted.astype(BF16).astype(F32)
-    mid = (weighted - hi).astype(BF16).astype(F32)
-    low = weighted - hi - mid
-    line = lax.broadcasted_iota(jnp.int32, (16, 512), 0)
-    three = jnp.where(line == 0, hi, jnp.where(line == 1, mid, jnp.where(line == 2, low, 0.0)))
-    moved = jnp.sum(mm(three.astype(BF16), wd[...]), axis=0, keepdims=True)
-    mine = lax.broadcasted_iota(jnp.int32, (8, 1), 0) == e
-    own0 = jnp.sum(jnp.where(mine, rg0, 0.0), axis=0, keepdims=True)
-    own1 = jnp.sum(jnp.where(mine, rg1, 0.0), axis=0, keepdims=True)
+    wt_out[...] = weighted
+    moved = jnp.sum(mm(three_rows(weighted, 512), wd[...]), axis=0, keepdims=True)
+    me_row = lax.broadcasted_iota(jnp.int32, (8, 1), 0) == e
+    own0 = jnp.sum(jnp.where(me_row, rg0, 0.0), axis=0, keepdims=True)
+    own1 = jnp.sum(jnp.where(me_row, rg1, 0.0), axis=0, keepdims=True)
     grad = moved + own0 * pool[0:1] + own1 * pool[1:2]
     for i in range(24):
         g_mine[i : i + 1] = grad[:, i * 128 : (i + 1) * 128]
-    total, more = all_sum(g_mine, g_exp, g_sum, g_seq, ge_s, ge_r, gq_s, gq_r)
-    gh_out[...] = total
-    for copy in sent + more:
+    gh_out[...], more = all_sum(g_mine, g_exp, g_sum, g_seq, ge_s, ge_r, gq_s, gq_r)
+
+    started = [home, vec_copy, *sent, *more, *q_z, *w_x, *w_y, *w_c, *far_w]
+    for group in (*kv_z, *near, *far, *rsc, *y_copies, *zc, *zd.values(), *xc):
+        started.extend(group)
+    for copy in started:
         copy.wait_send()
 
 
-def final(hs, pool, vec, head, wd, chosen, rejected):
+def layer(lengths, q, k, v, op, res, gain, router_t, routes, w_gate, w_up, w_down, head, pairs):
     vmem = pl.BlockSpec(memory_space=pltpu.VMEM)
+    hbm = pl.BlockSpec(memory_space=pl.ANY)
     dma = pltpu.SemaphoreType.DMA
     return pl.pallas_call(
-        final_kernel,
+        layer_kernel,
         out_shape=(
-            jax.ShapeDtypeStruct((16, 128), F32),
-            jax.ShapeDtypeStruct((8, 128), F32),
+            jax.ShapeDtypeStruct((EXPERTS, SEQS), F32),
+            jax.ShapeDtypeStruct((1, 1), F32),
             jax.ShapeDtypeStruct((24, 128), F32),
-            jax.ShapeDtypeStruct((8, 512), F32),
+            jax.ShapeDtypeStruct((1, 512), F32),
         ),
-        in_specs=[vmem] * 7,
+        in_specs=[pl.BlockSpec(memory_space=pltpu.SMEM)] + [hbm] * 4 + [vmem] * 4 + [hbm] * 3 + [vmem] * 2,
         out_specs=(vmem,) * 4,
         scratch_shapes=[
+            pltpu.VMEM((4, TOK, 1024), BF16),
+            pltpu.VMEM((4, 512, 256), BF16),
+            pltpu.VMEM((4, 512, 256), BF16),
+            pltpu.VMEM((4, TOK, 1024), BF16),
+            pltpu.VMEM((1024, D), BF16),
+            pltpu.VMEM((CHUNKS, 6, TOK, BLK), BF16),
+            pltpu.VMEM((CHUNKS, 6, TOK, BLK), BF16),
+            pltpu.VMEM((TOK, D), F32),
+            pltpu.VMEM((TOK, D), BF16),
+            pltpu.VMEM((ROWS, WIDE), BF16),
+            pltpu.VMEM((EXPERTS, 16, 128 * (CHUNKS + 1)), BF16),
+            pltpu.VMEM((EXPERTS, 16, 128 * (CHUNKS + 1)), BF16),
+            pltpu.VMEM((8, ROWS, WIDE), BF16),
+            pltpu.VMEM((4, D, 256), BF16),
+            pltpu.VMEM((4, D, 256), BF16),
+            pltpu.VMEM((4, EXT, 256), F32),
+            pltpu.VMEM((2, 16, 256), F32),
+            dma((10 + 2 * CHUNKS,)),
+            dma((3, 3)), dma((3, 3)),
+            dma((6, 4)), dma((6, 4)),
+            dma((19,)), dma((19,)),
+            dma((CHUNKS, 6)), dma((CHUNKS, 6)),
+            dma((4,)), dma((4,)),
+            dma((CHUNKS, 2, 7)), dma((CHUNKS, 2, 7)),
+            dma((CHUNKS, 4)), dma((CHUNKS, 4)),
+            dma((max(1, len(X_FIRST)), 4)), dma((max(1, len(X_FIRST)), 4)),
+            dma((CHUNKS, 4)), dma((CHUNKS, 4)),
+            dma, dma,
+            pltpu.VMEM((512, D), BF16), pltpu.VMEM((8, 512), F32), pltpu.VMEM((8, 512), F32), dma, dma, pltpu.VMEM((8, D), F32),
             pltpu.VMEM((16, 128), F32), pltpu.VMEM((7, 16, 128), F32),
             pltpu.VMEM((16, 128), F32), pltpu.VMEM((15, 16, 128), F32),
             pltpu.VMEM((24, 128), F32), pltpu.VMEM((7, 24, 128), F32),
@@ -725,29 +736,27 @@
             dma((7,)), dma((7,)), dma((15,)), dma((15,)),
         ],
         compiler_params=pltpu.CompilerParams(
-            collective_id=1, has_side_effects=True, vmem_limit_bytes=VMEM_LIMIT
+            collective_id=0, has_side_effects=True, vmem_limit_bytes=VMEM_LIMIT
         ),
-        name="final",
-    )(hs, pool, vec, head, wd, chosen, rejected)
+        cost_estimate=pl.CostEstimate(
+            flops=36_000_000_000, bytes_accessed=24_000_000, transcendentals=8_000_000
+        ),
+        name="layer",
+    )(lengths, q, k, v, op, res, gain, router_t, routes, w_gate, w_up, w_down, head, pairs)
 
 
 def per_device(
     query_states, key_states, value_states, residual, out_proj, norm_gain, router,
     w_gate, w_up, w_down, reward_head, lengths, routes, pair_list,
 ):
-    vec = jnp.sum(w_down[0].astype(F32) * reward_head[None, :], axis=1)[None, :]
-    hs, pool = layer(
+    pairs = jnp.pad(pair_list.reshape(8, 8), ((0, 0), (0, 120)))
+    rewards, loss, gh, wt = layer(
         lengths, query_states[0], key_states[0], value_states[0], out_proj, residual[0],
-        norm_gain[None, :], router.T, routes[0], w_gate[0], w_up[0],
+        norm_gain[None, :], router.T, routes[0], w_gate[0], w_up[0], w_down[0],
+        reward_head[None, :], pairs,
     )
-    pad = ((0, 0), (0, 124))
-    rew, loss, gh, wt = final(
-        hs, pool, vec, reward_head[None, :], w_down[0],
-        jnp.pad(pair_list[:, :, 0], pad), jnp.pad(pair_list[:, :, 1], pad),
-    )
-    rewards = rew[:, 0].reshape(2, 8).T
     grad_down = (wt[0][:, None] * reward_head[None, :]).astype(BF16)[None]
-    return rewards, loss[0, 0], gh.reshape(-1), grad_down
+    return rewards, loss.reshape(()), gh.reshape(-1), grad_down
 
 
 def solution(mesh):

time: 227 us -> 214 us (0.943)
  Pallas kernels: 214 us -> 203 us
  other arithmetic: 5.52 us -> 3 us
    pallas_call x2 -> x1, Pallas kernels: 214 us -> 203 us  [layer(): pl.pallas_call(layer_kernel, out_shape=(jax.ShapeDtypeStruct((EXPERTS, SE...]
    reduce_sum x1 -> x0, other arithmetic: 3.18 us -> none  [per_device(): vec = jnp.sum(w_down[0].astype(F32) * reward_head[None, :], axis=1)[None, :]]
    slice x4 -> x0, local copies, waits for them, and re-layouts: 2.72 us -> none  [the longest x1 1.19 us: per_device(): return (rewards, loss[0, 0], gh.reshape(-1), grad_down)]
where the time goes in v3:
time: 214 us; the launch traced here: 213 us
  Pallas kernels  203 us (95%)
  local copies, waits for them, and re-layouts  4.69 us (2%)
  other arithmetic  3 us (1%)
  between operations  2.35 us (1%)
    pallas_call x1, Pallas kernels, layer(): pl.pallas_call(layer_kernel, out_shape=(jax.ShapeDtypeStruct((EXPERTS, SE...  203 us

profile of v3, /device:TPU:0, one launch (start us, length us, event | category | flops | bytes accessed | tf_op | source)
XLA Modules:
  0.0 213.3 jit_solution(15234430538229714772)
XLA Ops:
  0.6 0.8 copy.19
  1.4 0.6 pad.4.pairs
  2.0 1.4 copy.18
  3.4 0.0 copy-start
  3.4 203.2 %layer.1 = (f32[8,2]{1,0:T(8,128)}, f32[1,1]{1,0:T(1,128)}, f32[24,128]{1,0:T(8,128)}, f32[1,512]{1,0:T(1,128)}) custom-call(s32[1,2]{1,0:T(1,128)} %len_ref.1, bf16[128,4096]{1,0:T(8,128)(2,1)} %bitcast.23, bf16[128,1024]{1,0:T(8,128)(2,1)} %bitcast.25, bf16[128,1024]{1,0:T(8,128)(2,1)} %bitcast.26, bf16[256,3072]{1,0:T(8,128)(2,1)} %op_ref.1, ...), custom_call_target="tpu_custom_call" | custom-call | flops 35999997952 | bytes 24000000 | tf_op jit(solution)/shard_map/layer/pallas_call | solution.py:691
  206.6 0.0 copy-start.1
  206.6 1.3 copy.20
  208.0 0.0 copy-done
  208.0 3.0 %multiply_convert_fusion = bf16[1,512,3072]{2,1,0:T(8,128)(2,1)} fusion(f32[3072]{0:T(1024)S(1)} %copy-done, f32[512]{0:T(512)} %bitcast.19), kind=kLoop, calls=%fused_computation | loop fusion | flops 3145728 | bytes 3160064 | tf_op jit(solution)/shard_map/convert_element_type | solution.py:758
  211.5 0.0 copy-done.1
  211.5 0.6 copy.24
Async XLA Ops:
  3.4 204.6 %copy-start = (f32[3072]{0:T(1024)S(1)}, f32[3072]{0:T(1024)}, u32[]{:S(2)}) copy-start(f32[3072]{0:T(1024)} %param.24) | copy-start | bytes 36868
  206.6 4.9 %copy-start.1 = (f32[24,128]{1,0:T(8,128)S(1)}, f32[24,128]{1,0:T(8,128)}, u32[]{:S(2)}) copy-start(f32[24,128]{1,0:T(8,128)} %get-tuple-element.10) | copy-start | bytes 36868

commit v4 on v3

--- a/solution.py
+++ b/solution.py
@@ -76,7 +76,7 @@
     rew_out, loss_out, gh_out, wt_out,
     qb, kb, vb, att, wb, part, rs, hid, nrm, stage, pack, unpack, xb, wg, wu, hs, hr,
     lsem, zs, zr, xs, xr, o_s, o_r, rs_s, rs_r, w_s, w_r, y_s, y_r, z_s, z_r, zd_s, zd_r,
-    x_s, x_r, h_s, h_r, wd, vec, vec_far, v_s, v_r, pool,
+    x_s, x_r, h_s, h_r, wd, vec, vec_far, v_s, v_r, kept, pool,
     r_mine, r_exp, r_sum, r_seq, g_mine, g_exp, g_sum, g_seq,
     re_s, re_r, rq_s, rq_r, ge_s, ge_r, gq_s, gq_r,
 ):
@@ -541,6 +541,29 @@
             return 0
 
         lax.fori_loop(low, high, chunk_step, 0)
+
+    def last_products(slot, start, stop):
+        span = slice(start * CW, stop * CW)
+
+        def chunk_step(c, _):
+            rows_x = xb[slot, :, span]
+            gate = mm(rows_x, wg[c, span])
+            up = mm(rows_x, wu[c, span])
+            if start:
+                gate = gate + kept[0, c]
+                up = up + kept[1, c]
+            if stop < CHUNKS:
+                kept[0, c] = gate
+                kept[1, c] = up
+            else:
+                ext = xb[slot, :, D:]
+                row_scale = ext[:, 16:17].astype(F32) + ext[:, 17:18].astype(F32)
+                gate = gate * row_scale
+                act = (gate / (1.0 + jnp.exp(-gate)) * (up * row_scale)).astype(BF16)
+                hs[c] = hs[c] + lhs_t(ext, act)
+            return 0
+
+        lax.fori_loop(0, 4, chunk_step, 0)
 
     w_y[4].wait_recv()
     w_y[5].wait_recv()
@@ -599,16 +622,20 @@
     pass_far(2)
     pass_far(3)
     experts(slot_of(3), 0, 4)
-    for d in (1, 3, 2):
-        if d == 2:
-            experts(slot_of(2), 0, 4)
+    for d in (1, 3):
         for c in range(CHUNKS):
             if c not in X_FIRST:
                 xc[c][d].wait_recv()
-            elif d == 2:
-                zd[c][2].wait_recv()
-                zd[c][3].wait_recv()
         experts(slot_of(d) + 1, 0, 4)
+    experts(slot_of(2), 0, 4)
+    zd[1][2].wait_recv()
+    zd[1][3].wait_recv()
+    xc[0][2].wait_recv()
+    last_products(slot_of(2) + 1, 0, 2)
+    xc[2][2].wait_recv()
+    last_products(slot_of(2) + 1, 2, 3)
+    xc[3][2].wait_recv()
+    last_products(slot_of(2) + 1, 3, 4)
 
     home = remote(hs.at[pl.ds(2, 2), pl.ds(0, 16)], hr, h_s, h_r, partner_w)
     home.start()
@@ -727,7 +754,8 @@
             dma((max(1, len(X_FIRST)), 4)), dma((max(1, len(X_FIRST)), 4)),
             dma((CHUNKS, 4)), dma((CHUNKS, 4)),
             dma, dma,
-            pltpu.VMEM((512, D), BF16), pltpu.VMEM((8, 512), F32), pltpu.VMEM((8, 512), F32), dma, dma, pltpu.VMEM((8, D), F32),
+            pltpu.VMEM((512, D), BF16), pltpu.VMEM((8, 512), F32), pltpu.VMEM((8, 512), F32), dma, dma,
+            pltpu.VMEM((2, 4, ROWS, 256), F32), pltpu.VMEM((8, D), F32),
             pltpu.VMEM((16, 128), F32), pltpu.VMEM((7, 16, 128), F32),
             pltpu.VMEM((16, 128), F32), pltpu.VMEM((15, 16, 128), F32),
             pltpu.VMEM((24, 128), F32), pltpu.VMEM((7, 24, 128), F32),

time: 214 us -> 215 us (level)
  no operation moved by 1% of the time
where the time goes in v4:
time: 215 us
  Pallas kernels  205 us (95%)
  local copies, waits for them, and re-layouts  4.69 us (2%)
  other arithmetic  3 us (1%)
  between operations  2.35 us (1%)
    pallas_call x1, Pallas kernels, layer(): pl.pallas_call(layer_kernel, out_shape=(jax.ShapeDtypeStruct((EXPERTS, SE...  205 us

profile of v4, /device:TPU:0, one launch (start us, length us, event | category | flops | bytes accessed | tf_op | source)
XLA Modules:
  0.0 214.6 jit_solution(725641156304322758)
XLA Ops:
  0.6 0.8 copy.19
  1.4 0.6 pad.4.pairs
  2.0 1.4 copy.18
  3.4 0.0 copy-start
  3.4 204.6 %layer.1 = (f32[8,2]{1,0:T(8,128)}, f32[1,1]{1,0:T(1,128)}, f32[24,128]{1,0:T(8,128)}, f32[1,512]{1,0:T(1,128)}) custom-call(s32[1,2]{1,0:T(1,128)} %len_ref.1, bf16[128,4096]{1,0:T(8,128)(2,1)} %bitcast.23, bf16[128,1024]{1,0:T(8,128)(2,1)} %bitcast.25, bf16[128,1024]{1,0:T(8,128)(2,1)} %bitcast.26, bf16[256,3072]{1,0:T(8,128)(2,1)} %op_ref.1, ...), custom_call_target="tpu_custom_call" | custom-call | flops 35999997952 | bytes 24000000 | tf_op jit(solution)/shard_map/layer/pallas_call | solution.py:718
  208.0 0.0 copy-start.1
  208.0 1.3 copy.20
  209.3 0.0 copy-done
  209.3 3.0 %multiply_convert_fusion = bf16[1,512,3072]{2,1,0:T(8,128)(2,1)} fusion(f32[3072]{0:T(1024)S(1)} %copy-done, f32[512]{0:T(512)} %bitcast.19), kind=kLoop, calls=%fused_computation | loop fusion | flops 3145728 | bytes 3160064 | tf_op jit(solution)/shard_map/convert_element_type | solution.py:786
  212.9 0.0 copy-done.1
  212.9 0.6 copy.24
Async XLA Ops:
  3.4 205.9 %copy-start = (f32[3072]{0:T(1024)S(1)}, f32[3072]{0:T(1024)}, u32[]{:S(2)}) copy-start(f32[3072]{0:T(1024)} %param.24) | copy-start | bytes 36868
  208.0 4.9 %copy-start.1 = (f32[24,128]{1,0:T(8,128)S(1)}, f32[24,128]{1,0:T(8,128)}, u32[]{:S(2)}) copy-start(f32[24,128]{1,0:T(8,128)} %get-tuple-element.10) | copy-start | bytes 36868
